TPU v7x, 256 devices: a whole 4x4x8 slice. The times are simulated.
256 devices in a mesh: ctx: 32 (over z, x_lo, core), tp: 8 (over x_hi, y).
Axes of the slice: x: 4 (x_hi: 2, x_lo: 2; x = x_hi * 2 + x_lo), y: 4, z: 8, core: 2. Of those that a mesh axis runs over, the one named last changes fastest.
Arguments:
- normed_rows: bfloat16 [4096, 5120], P('ctx', 'tp'), may hold values from -6 to 6
- query_rows: bfloat16 [4096, 3072], P('ctx', 'tp'), may hold values from -5 to 5
- key_rows: bfloat16 [4096, 3072], P('ctx', 'tp'), may hold values from -5 to 5
- value_rows: bfloat16 [4096, 3072], P('ctx', 'tp'), may hold values from -6 to 6
- grad_output: bfloat16 [4096, 3072], P('ctx', 'tp'), may hold values from -6 to 6
- stretch_ids: int32 [16], replicated, may hold values from 0 to 7, never falling along the last dimension, each value on 1 to 4 neighbouring positions
Outputs:
- query_grad: bfloat16 [5120, 3072], P('ctx', 'tp')
- key_grad: bfloat16 [5120, 3072], P('ctx', 'tp')
- value_grad: bfloat16 [5120, 3072], P('ctx', 'tp')
Inputs may be any that keep to these rules, and one draw needn't show every extreme that they name: `stretch_ids`: never falls from block to block; each stretch spans 1 to 4 consecutive blocks of 256 tokens, and some stretch exactly 4; every number of the range is used.
All inputs are finite; a program needn't handle non-finite values.
Results may differ from a plain program's by a relative error of at most 0.0075.
Values may be sent and summed in bfloat16 or wider, within the bound.
No kernel may reach another device: no remote copies, remote signals or barrier semaphores. Data moves between devices by JAX's collectives and lax.ppermute only.
A program may use at most 128 MiB of HBM per device.

v0:
```python
import functools
import math

import jax
import jax.numpy as jnp
from jax import lax
from jax.experimental import pallas as pl
from jax.experimental.pallas import tpu as pltpu
from jax.sharding import PartitionSpec as P

HD = 128
HEADS_DEV = 3
W = HD * HEADS_DEV
ROWS = 128
PLANES = 8
FACTOR = HD ** (-0.5)
SCALE2 = FACTOR * math.log2(math.e)
LOW = -1e30
F32 = jnp.float32
BF16 = jnp.bfloat16

CTX = 32
CORE_SWAP = [(i, i ^ 1) for i in range(CTX)]
X_SWAP = [(i, i ^ 2) for i in range(CTX)]
DIAG_SWAP = [(i, i ^ 3) for i in range(CTX)]
Z_UP = [(i, (i + 4) % CTX) for i in range(CTX)]
Z_DOWN = [(i, (i - 4) % CTX) for i in range(CTX)]
Z_GROUPS = [[4 * z + j for z in range(PLANES)] for j in range(4)]
TP_X = [(t, t ^ 4) for t in range(8)]
TP_UP = [(t, (t // 4) * 4 + (t + 1) % 4) for t in range(8)]
TP_DOWN = [(t, (t // 4) * 4 + (t + 3) % 4) for t in range(8)]
PLACES = [(z, j, t) for z in range(8) for j in range(4) for t in range(8)]
TURN_TP = [((4 * z + j) * 8 + t, (4 * z + j) * 8 + (t + z) % 8) for z, j, t in PLACES]
TURN_Z = [((4 * z + j) * 8 + t, (4 * ((t - z) % 8) + j) * 8 + t) for z, j, t in PLACES]

NT = (((1,), (1,)), ((), ()))
TN = (((0,), (0,)), ((), ()))
NN = (((1,), (0,)), ((), ()))


def dot(a, b, dims):
    return lax.dot_general(a, b, dims, preferred_element_type=F32)


RING_SHIFT = (0, -1, 1, -2, 2, -3, 3, 4)


def fill(scratch, refs):
    at = 0
    for ref in refs:
        n = ref.shape[0]
        scratch[at : at + n, :] = ref[...]
        at += n


def lane_row(values, width=ROWS):
    return jnp.concatenate([jnp.full((1, width), v, jnp.int32) for v in values], axis=1)


def fold(x, op):
    y = x.reshape(x.shape[0] // 8, 8, x.shape[1])
    return op(y, axis=0)


def plane_tables(place):
    z, xl = place[0], place[1]
    own = place[4 + 2 * z + xl]
    other = place[4 + 2 * z + 1 - xl]
    return [own, own, other, other]


def ring_tables(place):
    z, xl = place[0], place[1]
    return [place[4 + 2 * lax.rem(z + s + PLANES, PLANES) + xl] for s in RING_SHIFT]


def stats_kernel(place, *refs):
    qg, kv_in, out, sent = refs[:4], refs[4:13], refs[13], refs[14]
    qc, kc, sc = refs[15:]
    fill(qc, qg)
    fill(kc, kv_in)
    q_row = lane_row(plane_tables(place))
    k_st = ring_tables(place)
    out[...] = jnp.zeros_like(out)
    for h in range(HEADS_DEV):
        cols = slice(h * HD, (h + 1) * HD)
        gcols = slice(W + h * HD, W + (h + 1) * HD)
        qh = qc[:, cols]
        gh = qc[:, gcols]
        top = jnp.full((8, 4 * ROWS), LOW, F32)
        for k in range(PLANES):
            rows = slice(k * ROWS, (k + 1) * ROWS)
            s = dot(kc[rows, cols], qh, NT) * SCALE2
            s = jnp.where(q_row >= k_st[k], s, LOW)
            sc[rows, :] = s
            top = jnp.maximum(top, fold(s, jnp.max))
        m = jnp.maximum(jnp.max(top, axis=0, keepdims=True), 0.1 * LOW)
        total = jnp.zeros((8, 4 * ROWS), F32)
        weighted = jnp.zeros((8, 4 * ROWS), F32)
        for k in range(PLANES):
            rows = slice(k * ROWS, (k + 1) * ROWS)
            dp = dot(kc[rows, gcols], gh, NT)
            e = jnp.exp2(sc[rows, :] - m)
            total = total + fold(e, jnp.sum)
            weighted = weighted + fold(e * dp, jnp.sum)
        total = jnp.sum(total, axis=0, keepdims=True)
        weighted = jnp.sum(weighted, axis=0, keepdims=True)
        some = total > 0.0
        out[h : h + 1, :] = jnp.where(some, m + jnp.log2(total), 0.1 * LOW)
        out[3 + h : 4 + h, :] = jnp.where(some, weighted / total, 0.0)
    j = 2 * place[1] + place[2]
    for r in range(4):
        piece = out[:, r * ROWS : (r + 1) * ROWS]
        for i in range(PLANES):
            sent[4 * i + lax.bitwise_xor(j, r), :, :] = piece


def combine(parts):
    lse = [p[0:3] for p in parts]
    top = jnp.maximum(jnp.maximum(lse[0], lse[1]), jnp.maximum(lse[2], lse[3]))
    weights = [jnp.exp2(x - top) for x in lse]
    total = weights[0] + weights[1] + weights[2] + weights[3]
    delta = sum(w * p[3:6] for w, p in zip(weights, parts))
    return top + jnp.log2(total), delta / total


def dquery_kernel(place, *refs):
    qg, kv_in, stats = refs[:4], refs[4:13], refs[13:17]
    keep, send = refs[17:19]
    qc, kc, ds = refs[19:]
    fill(qc, qg)
    fill(kc, kv_in)
    q_row = lane_row(plane_tables(place))
    k_st = ring_tables(place)
    parts = []
    for d, ref in enumerate(stats):
        full = ref[...]
        parts.append(
            jnp.concatenate(
                [full[:, (r ^ d) * ROWS : ((r ^ d) + 1) * ROWS] for r in range(4)], axis=1
            )
        )
    all_lse, all_delta = combine(parts)
    for h in range(HEADS_DEV):
        cols = slice(h * HD, (h + 1) * HD)
        gcols = slice(W + h * HD, W + (h + 1) * HD)
        qh = qc[:, cols]
        gh = qc[:, gcols]
        lse = all_lse[h : h + 1, :]
        delta = all_delta[h : h + 1, :]
        for k in range(PLANES):
            rows = slice(k * ROWS, (k + 1) * ROWS)
            s = dot(kc[rows, cols], qh, NT) * SCALE2
            p = jnp.where(q_row >= k_st[k], jnp.exp2(s - lse), 0.0)
            dp = dot(kc[rows, gcols], gh, NT)
            ds[rows, :] = (FACTOR * p * (dp - delta)).astype(BF16)
        dq = dot(kc[:, cols], ds[...], TN).T
        for r in range(4):
            piece = dq[r * ROWS : (r + 1) * ROWS, :]
            if r % 2 == 0:
                keep[r // 2, :, cols] = piece
            else:
                send[r // 2, :, cols] = piece.astype(BF16)


def dkey_kernel(place, *refs):
    kv, qg, stats = refs[:4], refs[4], refs[5]
    keep, send = refs[6:]
    z, xl = place[0], place[1]
    q_row = lane_row([place[4 + 2 * i + xl] for i in range(PLANES)])
    k_st = plane_tables(place)
    all_lse, all_delta = combine(
        [jnp.concatenate([stats[4 * i + j] for i in range(PLANES)], axis=1) for j in range(4)]
    )
    for h in range(HEADS_DEV):
        cols = slice(h * HD, (h + 1) * HD)
        vcols = slice(W + h * HD, W + (h + 1) * HD)
        qh = qg[:, cols]
        gh = qg[:, vcols]
        lse = all_lse[h : h + 1, :]
        delta = all_delta[h : h + 1, :]
        for r in range(4):
            s = dot(kv[r][:, cols], qh, NT) * SCALE2
            p = jnp.where(q_row >= k_st[r], jnp.exp2(s - lse), 0.0)
            dp = dot(kv[r][:, vcols], gh, NT)
            ds = (FACTOR * p * (dp - delta)).astype(BF16)
            dv = dot(p.astype(BF16), gh, NN)
            dk = dot(ds, qh, NN)
            if r % 2 == 0:
                keep[r // 2, :, cols] = dk
                keep[r // 2, :, vcols] = dv
            else:
                send[r // 2, :, cols] = dk.astype(BF16)
                send[r // 2, :, vcols] = dv.astype(BF16)


def normed_kernel(place, pair, up, down, up2, down2, out):
    z, t = place[0], place[3]
    y = lax.rem(t, 4)
    xh = lax.div(t, 4)

    def put(block, hi, yy):
        plane = lax.rem(hi * 4 + lax.rem(yy + 4, 4) - z + PLANES, PLANES)
        out[:, pl.ds(pl.multiple_of(plane * ROWS, ROWS), ROWS)] = block.T

    for ref, dy in ((pair, 0), (up, -1), (down, 1)):
        put(ref[:ROWS, :], xh, y + dy)
        put(ref[ROWS:, :], 1 - xh, y + dy)
    put(up2[...], xh, y - 2)
    put(down2[...], 1 - xh, y + 2)


def product(place, at, b, keep, send):
    core = place[2]
    for half in range(2):
        mine = pl.multiple_of((2 * half + core) * 160, 160)
        theirs = pl.multiple_of((2 * half + 1 - core) * 160, 160)
        keep[half, :, :] = dot(at[pl.ds(mine, 160), :], b[...], NN)
        send[half, :, :] = dot(at[pl.ds(theirs, 160), :], b[...], NN).astype(BF16)


def call(kernel, out_shape, *args, scratch=(), smem=0, flops=0, name=None):
    specs = [pl.BlockSpec(memory_space=pltpu.SMEM)] * smem
    specs += [pl.BlockSpec(memory_space=pltpu.VMEM)] * (len(args) - smem)
    size = sum(math.prod(a.shape) * a.dtype.itemsize for a in args)
    return pl.pallas_call(
        kernel,
        out_shape=out_shape,
        in_specs=specs,
        out_specs=jax.tree.map(lambda _: pl.BlockSpec(memory_space=pltpu.VMEM), out_shape),
        scratch_shapes=list(scratch),
        compiler_params=pltpu.CompilerParams(vmem_limit_bytes=40 * 2**20),
        cost_estimate=pl.CostEstimate(flops=flops, bytes_accessed=size if flops else 0, transcendentals=0),
        name=name,
    )(*args)


def shaped(shape, dtype):
    return jax.ShapeDtypeStruct(shape, dtype)


def plane_gather(part):
    across = lax.ppermute(part, "ctx", X_SWAP)
    beside = lax.ppermute(part, "ctx", CORE_SWAP)
    diag = lax.ppermute(across, "ctx", CORE_SWAP)
    return [part, beside, across, diag]


def row_sum(keep, send, xl):
    got = lax.ppermute(send, "ctx", CORE_SWAP).astype(F32)
    both = keep + got
    mine = lax.dynamic_index_in_dim(both, xl, 0, keepdims=False)
    other = lax.dynamic_index_in_dim(both, 1 - xl, 0, keepdims=False).astype(BF16)
    return mine + lax.ppermute(other, "ctx", X_SWAP).astype(F32)


def after(value, *earlier):
    return lax.optimization_barrier((value, *earlier))[0]


def shards(normed_rows, query_rows, key_rows, value_rows, grad_output, stretch_ids):
    ctx = lax.axis_index("ctx")
    xl = lax.rem(lax.div(ctx, 2), 2)
    place = jnp.concatenate(
        [
            jnp.stack([lax.div(ctx, 4), xl, lax.rem(ctx, 2), lax.axis_index("tp")]).astype(
                jnp.int32
            ),
            stretch_ids,
        ]
    )
    half = ROWS // 2
    kv_own = jnp.concatenate([key_rows, value_rows], axis=1)
    qg_own = jnp.concatenate([query_rows, grad_output], axis=1)

    up1 = lax.ppermute(kv_own, "ctx", Z_UP)
    down1 = lax.ppermute(kv_own, "ctx", Z_DOWN)
    qg_plane = plane_gather(qg_own)
    turned_tp = lax.ppermute(normed_rows, ("ctx", "tp"), TURN_TP)
    up1, down1 = lax.optimization_barrier((up1, down1))
    up2 = lax.ppermute(up1, "ctx", Z_UP)
    down2 = lax.ppermute(down1, "ctx", Z_DOWN)
    up2, down2, qg_sent, turned_tp = lax.optimization_barrier((up2, down2, qg_own, turned_tp))
    qg_all = lax.all_gather(qg_sent, "ctx", axis=0, tiled=True, axis_index_groups=Z_GROUPS)
    up3 = lax.ppermute(up2, "ctx", Z_UP)
    down3 = lax.ppermute(down2, "ctx", Z_DOWN)
    up3, down3, kv_later, turned_tp = lax.optimization_barrier((up3, down3, kv_own, turned_tp))
    far_a = lax.ppermute(up3[:half], "ctx", Z_UP)
    far_b = lax.ppermute(down3[half:], "ctx", Z_DOWN)
    kv_plane = plane_gather(kv_later)
    kv_ring = [kv_own, up1, down1, up2, down2, up3, down3, far_a, far_b]

    wide = [
        pltpu.VMEM((4 * ROWS, 2 * W), BF16),
        pltpu.VMEM((PLANES * ROWS, 2 * W), BF16),
    ]
    stats, stats_sent = call(
        stats_kernel,
        (shaped((8, 4 * ROWS), F32), shaped((CTX, 8, ROWS), F32)),
        place,
        *qg_plane,
        *kv_ring,
        smem=1,
        scratch=wide + [pltpu.VMEM((PLANES * ROWS, 4 * ROWS), F32)],
        flops=2 * 2 * 1024 * 512 * W,
        name="softmax_statistics",
    )
    all_stats = lax.all_to_all(stats_sent, "ctx", split_axis=0, concat_axis=0, tiled=True)
    dq_keep, dq_send = call(
        dquery_kernel,
        (shaped((2, ROWS, W), F32), shaped((2, ROWS, W), BF16)),
        place,
        *qg_plane,
        *kv_ring,
        stats,
        lax.ppermute(stats, "ctx", CORE_SWAP),
        lax.ppermute(stats, "ctx", X_SWAP),
        lax.ppermute(stats, "ctx", DIAG_SWAP),
        smem=1,
        scratch=wide + [pltpu.VMEM((PLANES * ROWS, 4 * ROWS), BF16)],
        flops=0,
        name="query_gradient",
    )
    dq_got = lax.ppermute(dq_send, "ctx", CORE_SWAP).astype(F32)
    dq_other = (dq_keep[1] + dq_got[1]).astype(BF16)
    dkv_keep, dkv_send = call(
        dkey_kernel,
        (shaped((2, ROWS, 2 * W), F32), shaped((2, ROWS, 2 * W), BF16)),
        place,
        *kv_plane,
        qg_all,
        after(all_stats, dq_send),
        smem=1,
        flops=4 * 2 * 1024 * 512 * W,
        name="key_value_gradient",
    )
    dkv_got = lax.ppermute(dkv_send, "ctx", CORE_SWAP).astype(F32)
    dkv_other = (dkv_keep[1] + dkv_got[1]).astype(BF16)
    dkv = (
        dkv_keep[0] + dkv_got[0] + lax.ppermute(dkv_other, "ctx", X_SWAP).astype(F32)
    ).astype(BF16)
    dq = (
        dq_keep[0] + dq_got[0] + lax.ppermute(dq_other, "ctx", X_SWAP).astype(F32)
    ).astype(BF16)
    moved = lax.ppermute(after(turned_tp, dkv_send), ("ctx", "tp"), TURN_Z)
    grads = jnp.concatenate([dq, dkv], axis=1)
    grads_all = lax.all_gather(grads, "ctx", axis=0, tiled=True, axis_index_groups=Z_GROUPS)

    moved_x = lax.ppermute(moved, "tp", TP_X)
    pair = jnp.concatenate([moved, moved_x], axis=0)
    n_up = lax.ppermute(pair, "tp", TP_UP)
    n_down = lax.ppermute(pair, "tp", TP_DOWN)
    turned = call(
        normed_kernel,
        shaped((640, PLANES * ROWS), BF16),
        place,
        pair,
        n_up,
        n_down,
        lax.ppermute(n_up[:ROWS], "tp", TP_UP),
        lax.ppermute(n_down[ROWS:], "tp", TP_DOWN),
        smem=1,
        name="normed_columns",
    )
    keep, send = call(
        product,
        (shaped((2, 160, 3 * W), F32), shaped((2, 160, 3 * W), BF16)),
        place,
        turned,
        grads_all,
        smem=1,
        flops=2 * 640 * 1024 * 3 * W,
        name="weight_product",
    )
    out = row_sum(keep, send, xl).astype(BF16)
    return (out[:, :W], out[:, W : 2 * W], out[:, 2 * W :])


def solution(mesh):
    return jax.shard_map(
        shards,
        mesh=mesh,
        in_specs=(
            P("ctx", "tp"),
            P("ctx", "tp"),
            P("ctx", "tp"),
            P("ctx", "tp"),
            P("ctx", "tp"),
            P(),
        ),
        out_specs=(P("ctx", "tp"), P("ctx", "tp"), P("ctx", "tp")),
        check_vma=False,
    )
```

profile of v0, /device:TPU:1, one launch (start us, length us, event | category | flops | bytes accessed | tf_op | source)
XLA Modules:
  0.0 153.5 jit_solution(16502036139715378863)
XLA Ops:
  7.2 0.9 constant_dynamic-update-slice_fusion.1
  8.1 0.9 constant_dynamic-update-slice_fusion.refs_4_.refs_0_
  9.0 2.5 %collective-permute-start = (bf16[128,768]{1,0:T(8,128)(2,1)S(1)}, bf16[128,768]{1,0:T(8,128)(2,1)S(1)}, u32[]{:S(2)}, u32[]{:S(2)}) collective-permute-start(bf16[128,768]{1,0:T(8,128)(2,1)S(1)} %constant_dynamic-update-slice_fusion.refs_4_.refs_0_), channel_id=1, source_target_pairs={{0,32},{8,40},{16,48},{24,56},{32,64},{40,72},{48,80},{56,88},{64,... | collective-permute-start | bytes 589832 | tf_op jit(solution)/shard_map/ppermute | solution.py:276
  11.6 4.0 %collective-permute-start.1 = (bf16[128,768]{1,0:T(8,128)(2,1)S(1)}, bf16[128,768]{1,0:T(8,128)(2,1)S(1)}, u32[]{:S(2)}, u32[]{:S(2)}) collective-permute-start(bf16[128,768]{1,0:T(8,128)(2,1)S(1)} %constant_dynamic-update-slice_fusion.refs_4_.refs_0_), channel_id=1, source_target_pairs={{0,224},{8,232},{16,240},{24,248},{32,0},{40,8},{48,16},{56,24},{6... | collective-permute-start | bytes 589832 | tf_op jit(solution)/shard_map/ppermute | solution.py:277
  15.6 1.6 %collective-permute-start.4 = (bf16[128,640]{1,0:T(8,128)(2,1)}, bf16[128,640]{1,0:T(8,128)(2,1)S(1)}, u32[]{:S(2)}, u32[]{:S(2)}) collective-permute-start(bf16[128,640]{1,0:T(8,128)(2,1)} %param.6), channel_id=1, source_target_pairs={{0,0},{1,1},{2,2},{3,3},{4,4},{5,5},{6,6},{7,7},{8,8},{9,9},{10,10... | collective-permute-start | bytes 491528 | tf_op jit(solution)/shard_map/ppermute | solution.py:279
  17.2 3.0 %collective-permute-done.refs_5_ = bf16[128,768]{1,0:T(8,128)(2,1)S(1)} collective-permute-done((bf16[128,768]{1,0:T(8,128)(2,1)S(1)}, bf16[128,768]{1,0:T(8,128)(2,1)S(1)}, u32[]{:S(2)}, u32[]{:S(2)}) %collective-permute-start) | collective-permute-done | bytes 196640 | tf_op jit(solution)/shard_map/ppermute | solution.py:276
  20.1 4.1 %collective-permute-start.3 = (bf16[128,768]{1,0:T(8,128)(2,1)S(1)}, bf16[128,768]{1,0:T(8,128)(2,1)S(1)}, u32[]{:S(2)}, u32[]{:S(2)}) collective-permute-start(bf16[128,768]{1,0:T(8,128)(2,1)S(1)} %collective-permute-done.1.refs_6_), channel_id=1, source_target_pairs={{0,224},{8,232},{16,240},{24,248},{32,0},{40,8},{48,16},{56,24},{6... | collective-permute-start | bytes 589832 | tf_op jit(solution)/shard_map/ppermute | solution.py:282
  24.3 0.9 constant_dynamic-update-slice_fusion.3
  25.2 0.9 constant_dynamic-update-slice_fusion.2.refs_0_
  26.1 1.8 %collective-permute-done.2.refs_7_ = bf16[128,768]{1,0:T(8,128)(2,1)S(1)} collective-permute-done((bf16[128,768]{1,0:T(8,128)(2,1)S(1)}, bf16[128,768]{1,0:T(8,128)(2,1)S(1)}, u32[]{:S(2)}, u32[]{:S(2)}) %collective-permute-start.2) | collective-permute-done | bytes 196640 | tf_op jit(solution)/shard_map/ppermute | solution.py:281
  28.8 2.2 %collective-permute-start.6 = (bf16[128,768]{1,0:T(8,128)(2,1)S(1)}, bf16[128,768]{1,0:T(8,128)(2,1)S(1)}, u32[]{:S(2)}, u32[]{:S(2)}) collective-permute-start(bf16[128,768]{1,0:T(8,128)(2,1)S(1)} %collective-permute-done.3.refs_8_), channel_id=1, source_target_pairs={{0,224},{8,232},{16,240},{24,248},{32,0},{40,8},{48,16},{56,24},{6... | collective-permute-start | bytes 589832 | tf_op jit(solution)/shard_map/ppermute | solution.py:286
  31.0 3.0 %collective-permute-start.10 = (bf16[128,768]{1,0:T(8,128)(2,1)}, bf16[128,768]{1,0:T(8,128)(2,1)S(1)}, u32[]{:S(2)}, u32[]{:S(2)}) collective-permute-start(bf16[128,768]{1,0:T(8,128)(2,1)} %copy-done), channel_id=1, source_target_pairs={{0,8},{8,0},{16,24},{24,16},{32,40},{40,32},{48,56},{56,48},{64,72... | collective-permute-start | bytes 589832 | tf_op jit(solution)/shard_map/ppermute | solution.py:244
  34.0 2.0 %collective-permute-start.12 = (bf16[128,768]{1,0:T(8,128)(2,1)S(1)}, bf16[128,768]{1,0:T(8,128)(2,1)S(1)}, u32[]{:S(2)}, u32[]{:S(2)}) collective-permute-start(bf16[128,768]{1,0:T(8,128)(2,1)S(1)} %collective-permute-done.11.refs_2_), channel_id=1, source_target_pairs={{0,8},{8,0},{16,24},{24,16},{32,40},{40,32},{48,56},{56,48},{64,72... | collective-permute-start | bytes 589832 | tf_op jit(solution)/shard_map/ppermute | solution.py:245
  36.5 2.5 %collective-permute-start.14 = (bf16[64,768]{1,0:T(8,128)(2,1)S(1)}, bf16[64,768]{1,0:T(8,128)(2,1)S(1)}, u32[]{:S(2)}, u32[]{:S(2)}) collective-permute-start(bf16[64,768]{1,0:T(8,128)(2,1)S(1)} %slice.46), channel_id=1, source_target_pairs={{0,224},{8,232},{16,240},{24,248},{32,0},{40,8},{48,16},{56,24},{6... | collective-permute-start | bytes 294920 | tf_op jit(solution)/shard_map/ppermute | solution.py:289
  40.1 0.8 collective-permute-done.13.refs_11_
  40.9 1.4 collective-permute-done.14.refs_12_
  42.3 0.9 copy-done.1
  43.2 4.2 %softmax_statistics.1 = (f32[8,512]{1,0:T(8,128)S(1)}, f32[32,8,128]{2,1,0:T(8,128)}) custom-call(s32[20]{0:T(128)S(1)} %concatenate.15.place, bf16[128,768]{1,0:T(8,128)(2,1)S(1)} %copy-done.1, bf16[128,768]{1,0:T(8,128)(2,1)S(1)} %collective-permute-done.10.refs_1_, bf16[128,768]{1,0:T(8,128)(2,1)S(1)} %collective-permute-done.11.refs_2_, ...), custom_call_target="tpu_custom_call" | custom-call | flops 805306368 | bytes 2359376 | tf_op jit(solution)/shard_map/softmax_statistics/pallas_call | solution.py:226
  47.4 10.1 %all-to-all-start = ((f32[32,8,128]{2,1,0:T(8,128)}), f32[32,8,128]{2,1,0:T(8,128)S(1)}, u32[]{:S(2)}, u32[]{:S(2)}) async-start(f32[32,8,128]{2,1,0:T(8,128)} %get-tuple-element.33), calls=%async_computation | async-start | bytes 262144 | tf_op jit(solution)/shard_map/all_to_all | solution.py:308
  58.6 1.3 collective-permute-start.16
  60.4 1.2 collective-permute-done.16.refs_15_
  61.5 2.0 %collective-permute-done.17.refs_16_ = f32[8,512]{1,0:T(8,128)S(1)} collective-permute-done((f32[8,512]{1,0:T(8,128)S(1)}, f32[8,512]{1,0:T(8,128)S(1)}, u32[]{:S(2)}, u32[]{:S(2)}) %collective-permute-start.17) | collective-permute-done | bytes 16416 | tf_op jit(solution)/shard_map/ppermute | solution.py:318
  63.6 3.7 %query_gradient.1 = (f32[2,128,384]{2,1,0:T(8,128)S(1)}, bf16[2,128,384]{2,1,0:T(8,128)(2,1)}) custom-call(s32[20]{0:T(128)S(1)} %concatenate.15.place, bf16[128,768]{1,0:T(8,128)(2,1)S(1)} %copy-done.2, bf16[128,768]{1,0:T(8,128)(2,1)S(1)} %collective-permute-done.10.refs_1_, bf16[128,768]{1,0:T(8,128)(2,1)S(1)} %collective-permute-done.11.refs_2_, ...), custom_call_target="tpu_custom_call" | custom-call | tf_op jit(solution)/shard_map/query_gradient/pallas_call | solution.py:226
  67.3 0.9 all-to-all-done.refs_5_
  68.2 1.4 copy-done.4
  69.6 4.2 %key_value_gradient.1 = (f32[2,128,768]{2,1,0:T(8,128)S(1)}, bf16[2,128,768]{2,1,0:T(8,128)(2,1)S(1)}) custom-call(s32[20]{0:T(128)S(1)} %concatenate.15.place, bf16[128,768]{1,0:T(8,128)(2,1)S(1)} %constant_dynamic-update-slice_fusion.refs_4_.refs_0_, bf16[128,768]{1,0:T(8,128)(2,1)S(1)} %collective-permute-done.7.refs_1_, ...), custom_call_target="tpu_custom_call" | custom-call | flops 1610612736 | bytes 2490448 | tf_op jit(solution)/shard_map/key_value_gradient/pallas_call | solution.py:226
  73.8 2.5 %collective-permute-start.26 = (bf16[2,128,768]{2,1,0:T(8,128)(2,1)S(1)}, bf16[2,128,768]{2,1,0:T(8,128)(2,1)S(1)}, u32[]{:S(2)}, u32[]{:S(2)}) collective-permute-start(bf16[2,128,768]{2,1,0:T(8,128)(2,1)S(1)} %get-tuple-element.37), channel_id=1, source_target_pairs={{0,8},{8,0},{16,24},{24,16},{32,40},{40,32},{48,56},{56,48},{64,72... | collective-permute-start | bytes 1179656 | tf_op jit(solution)/shard_map/ppermute | solution.py:337
  76.4 1.4 collective-permute-start.25
  77.9 1.3 collective-permute-start.27
  79.2 1.7 %collective-permute-done.25 = bf16[128,384]{1,0:T(8,128)(2,1)S(1)} collective-permute-done((bf16[128,384]{1,0:T(8,128)(2,1)S(1)}, bf16[128,384]{1,0:T(8,128)(2,1)S(1)}, u32[]{:S(2)}, u32[]{:S(2)}) %collective-permute-start.25) | collective-permute-done | bytes 98336 | tf_op jit(solution)/shard_map/ppermute | solution.py:343
  80.9 4.2 %collective-permute-done.27 = bf16[128,768]{1,0:T(8,128)(2,1)S(1)} collective-permute-done((bf16[128,768]{1,0:T(8,128)(2,1)S(1)}, bf16[128,768]{1,0:T(8,128)(2,1)S(1)}, u32[]{:S(2)}, u32[]{:S(2)}) %collective-permute-start.27) | collective-permute-done | bytes 196640 | tf_op jit(solution)/shard_map/ppermute | solution.py:340
  86.6 12.9 %collective-permute-start.19 = (bf16[128,640]{1,0:T(8,128)(2,1)S(1)}, bf16[128,640]{1,0:T(8,128)(2,1)S(1)}, u32[]{:S(2)}, u32[]{:S(2)}) collective-permute-start(bf16[128,640]{1,0:T(8,128)(2,1)S(1)} %collective-permute-done.18), channel_id=1, source_target_pairs={{0,4},{1,5},{2,6},{3,7},{4,0},{5,1},{6,2},{7,3},{8,12},{9,13},{10,... | collective-permute-start | bytes 491528 | tf_op jit(solution)/shard_map/ppermute | solution.py:349
  99.5 2.7 %collective-permute-done.19 = bf16[128,640]{1,0:T(8,128)(2,1)S(1)} collective-permute-done((bf16[128,640]{1,0:T(8,128)(2,1)S(1)}, bf16[128,640]{1,0:T(8,128)(2,1)S(1)}, u32[]{:S(2)}, u32[]{:S(2)}) %collective-permute-start.19) | collective-permute-done | bytes 163872 | tf_op jit(solution)/shard_map/ppermute | solution.py:349
  102.3 1.6 %collective-permute-start.20 = (bf16[256,640]{1,0:T(8,128)(2,1)S(1)}, bf16[256,640]{1,0:T(8,128)(2,1)S(1)}, u32[]{:S(2)}, u32[]{:S(2)}) collective-permute-start(bf16[256,640]{1,0:T(8,128)(2,1)S(1)} %constant_dynamic-update-slice_fusion.4.pair), channel_id=1, source_target_pairs={{0,1},{1,2},{2,3},{3,0},{4,5},{5,6},{6,7},{7,4},{8,9},{9,10},{10,1... | collective-permute-start | bytes 983048 | tf_op jit(solution)/shard_map/ppermute | solution.py:351
  103.9 1.6 %collective-permute-start.21 = (bf16[256,640]{1,0:T(8,128)(2,1)S(1)}, bf16[256,640]{1,0:T(8,128)(2,1)S(1)}, u32[]{:S(2)}, u32[]{:S(2)}) collective-permute-start(bf16[256,640]{1,0:T(8,128)(2,1)S(1)} %constant_dynamic-update-slice_fusion.4.pair), channel_id=1, source_target_pairs={{0,3},{1,0},{2,1},{3,2},{4,7},{5,4},{6,5},{7,6},{8,11},{9,8},{10,9... | collective-permute-start | bytes 983048 | tf_op jit(solution)/shard_map/ppermute | solution.py:352
  105.5 4.8 %collective-permute-done.20.up = bf16[256,640]{1,0:T(8,128)(2,1)S(1)} collective-permute-done((bf16[256,640]{1,0:T(8,128)(2,1)S(1)}, bf16[256,640]{1,0:T(8,128)(2,1)S(1)}, u32[]{:S(2)}, u32[]{:S(2)}) %collective-permute-start.20) | collective-permute-done | bytes 327712 | tf_op jit(solution)/shard_map/ppermute | solution.py:351
  110.8 2.3 %collective-permute-start.23 = (bf16[128,640]{1,0:T(8,128)(2,1)S(1)}, bf16[128,640]{1,0:T(8,128)(2,1)S(1)}, u32[]{:S(2)}, u32[]{:S(2)}) collective-permute-start(bf16[128,640]{1,0:T(8,128)(2,1)S(1)} %slice.61), channel_id=1, source_target_pairs={{0,3},{1,0},{2,1},{3,2},{4,7},{5,4},{6,5},{7,6},{8,11},{9,8},{10,9... | collective-permute-start | bytes 491528 | tf_op jit(solution)/shard_map/ppermute | solution.py:361
  113.1 3.0 %collective-permute-done.22.up2 = bf16[128,640]{1,0:T(8,128)(2,1)S(1)} collective-permute-done((bf16[128,640]{1,0:T(8,128)(2,1)S(1)}, bf16[128,640]{1,0:T(8,128)(2,1)S(1)}, u32[]{:S(2)}, u32[]{:S(2)}) %collective-permute-start.22) | collective-permute-done | bytes 163872 | tf_op jit(solution)/shard_map/ppermute | solution.py:360
  116.1 1.0 normed_columns.1.at
  117.1 6.8 %all-gather.5.cloned.1.call-done.b = bf16[1024,1152]{1,0:T(8,128)(2,1)} async-done(((bf16[128,1152]{1,0:T(8,128)(2,1)}), bf16[1024,1152]{1,0:T(8,128)(2,1)}) %all-gather.5.cloned.1.call-update) | async-done | bytes 2359312 | tf_op jit(solution)/shard_map/all_gather | solution.py:347
  123.9 1.7 %copy-done.3 = bf16[1024,1152]{1,0:T(8,128)(2,1)S(1)} copy-done((bf16[1024,1152]{1,0:T(8,128)(2,1)S(1)}, bf16[1024,1152]{1,0:T(8,128)(2,1)}, u32[]{:S(2)}) %copy-start.3) | copy-done | bytes 2359320
  125.5 3.3 %weight_product.1 = (f32[2,160,1152]{2,1,0:T(8,128)S(1)}, bf16[2,160,1152]{2,1,0:T(8,128)(2,1)}) custom-call(s32[20]{0:T(128)S(1)} %concatenate.15.place, bf16[640,1024]{1,0:T(8,128)(2,1)S(1)} %normed_columns.1.at, bf16[1024,1152]{1,0:T(8,128)(2,1)S(1)} %copy-done.3), custom_call_target="tpu_custom_call" | custom-call | flops 1509949440 | bytes 3670096 | tf_op jit(solution)/shard_map/weight_product/pallas_call | solution.py:226
  128.8 3.6 %collective-permute-start.28 = (bf16[2,160,1152]{2,1,0:T(8,128)(2,1)}, bf16[2,160,1152]{2,1,0:T(8,128)(2,1)}, u32[]{:S(2)}, u32[]{:S(2)}) collective-permute-start(bf16[2,160,1152]{2,1,0:T(8,128)(2,1)} %get-tuple-element.42), channel_id=1, source_target_pairs={{0,8},{8,0},{16,24},{24,16},{32,40},{40,32},{48,56},{56,48},{64,72... | collective-permute-start | bytes 2211848 | tf_op jit(solution)/shard_map/ppermute | solution.py:250
  132.4 2.2 %collective-permute-done.28 = bf16[2,160,1152]{2,1,0:T(8,128)(2,1)} collective-permute-done((bf16[2,160,1152]{2,1,0:T(8,128)(2,1)}, bf16[2,160,1152]{2,1,0:T(8,128)(2,1)}, u32[]{:S(2)}, u32[]{:S(2)}) %collective-permute-start.28) | collective-permute-done | bytes 737312 | tf_op jit(solution)/shard_map/ppermute | solution.py:250
  134.6 1.2 convert_add_fusion
  135.9 1.3 collective-permute-start.29
  137.2 8.6 %collective-permute-done.29 = bf16[160,1152]{1,0:T(8,128)(2,1)S(1)} collective-permute-done((bf16[160,1152]{1,0:T(8,128)(2,1)S(1)}, bf16[160,1152]{1,0:T(8,128)(2,1)S(1)}, u32[]{:S(2)}, u32[]{:S(2)}) %collective-permute-start.29) | collective-permute-done | bytes 368672 | tf_op jit(solution)/shard_map/ppermute | solution.py:254
  145.9 0.7 fusion.12
  (61 shorter events, 6.3 us)
Async XLA Ops:
  7.2 61.0 %all-gather.3.cloned.1.call-start = ((), (), s32[]{:S(2)}) async-start(), calls=%async_computation.1 | async-start | bytes 1769472 | tf_op jit(solution)/shard_map/all_gather | solution.py:284
  9.0 11.1 %collective-permute-start = (bf16[128,768]{1,0:T(8,128)(2,1)S(1)}, bf16[128,768]{1,0:T(8,128)(2,1)S(1)}, u32[]{:S(2)}, u32[]{:S(2)}) collective-permute-start(bf16[128,768]{1,0:T(8,128)(2,1)S(1)} %constant_dynamic-update-slice_fusion.refs_4_.refs_0_), channel_id=1, source_target_pairs={{0,32},{8,40},{16,48},{24,56},{32,64},{40,72},{48,80},{56,88},{64,... | collective-permute-start | bytes 589832 | tf_op jit(solution)/shard_map/ppermute | solution.py:276
  11.6 8.6 %collective-permute-start.1 = (bf16[128,768]{1,0:T(8,128)(2,1)S(1)}, bf16[128,768]{1,0:T(8,128)(2,1)S(1)}, u32[]{:S(2)}, u32[]{:S(2)}) collective-permute-start(bf16[128,768]{1,0:T(8,128)(2,1)S(1)} %constant_dynamic-update-slice_fusion.refs_4_.refs_0_), channel_id=1, source_target_pairs={{0,224},{8,232},{16,240},{24,248},{32,0},{40,8},{48,16},{56,24},{6... | collective-permute-start | bytes 589832 | tf_op jit(solution)/shard_map/ppermute | solution.py:277
  15.6 10.5 %collective-permute-start.4 = (bf16[128,640]{1,0:T(8,128)(2,1)}, bf16[128,640]{1,0:T(8,128)(2,1)S(1)}, u32[]{:S(2)}, u32[]{:S(2)}) collective-permute-start(bf16[128,640]{1,0:T(8,128)(2,1)} %param.6), channel_id=1, source_target_pairs={{0,0},{1,1},{2,2},{3,3},{4,4},{5,5},{6,6},{7,7},{8,8},{9,9},{10,10... | collective-permute-start | bytes 491528 | tf_op jit(solution)/shard_map/ppermute | solution.py:279
  20.1 7.7 %collective-permute-start.2 = (bf16[128,768]{1,0:T(8,128)(2,1)S(1)}, bf16[128,768]{1,0:T(8,128)(2,1)S(1)}, u32[]{:S(2)}, u32[]{:S(2)}) collective-permute-start(bf16[128,768]{1,0:T(8,128)(2,1)S(1)} %collective-permute-done.refs_5_), channel_id=1, source_target_pairs={{0,32},{8,40},{16,48},{24,56},{32,64},{40,72},{48,80},{56,88},{64,... | collective-permute-start | bytes 589832 | tf_op jit(solution)/shard_map/ppermute | solution.py:281
  20.1 7.7 %collective-permute-start.3 = (bf16[128,768]{1,0:T(8,128)(2,1)S(1)}, bf16[128,768]{1,0:T(8,128)(2,1)S(1)}, u32[]{:S(2)}, u32[]{:S(2)}) collective-permute-start(bf16[128,768]{1,0:T(8,128)(2,1)S(1)} %collective-permute-done.1.refs_6_), channel_id=1, source_target_pairs={{0,224},{8,232},{16,240},{24,248},{32,0},{40,8},{48,16},{56,24},{6... | collective-permute-start | bytes 589832 | tf_op jit(solution)/shard_map/ppermute | solution.py:282
  26.1 1.8 %copy-start = (bf16[128,768]{1,0:T(8,128)(2,1)}, bf16[128,768]{1,0:T(8,128)(2,1)S(1)}, u32[]{:S(2)}) copy-start(bf16[128,768]{1,0:T(8,128)(2,1)S(1)} %constant_dynamic-update-slice_fusion.2.refs_0_) | copy-start | bytes 589828
  26.1 1.8 %copy-start.5 = (bf16[128,640]{1,0:T(8,128)(2,1)}, bf16[128,640]{1,0:T(8,128)(2,1)S(1)}, u32[]{:S(2)}) copy-start(bf16[128,640]{1,0:T(8,128)(2,1)S(1)} %collective-permute-done.4) | copy-start | bytes 491524
  27.9 6.1 %collective-permute-start.11 = (bf16[128,768]{1,0:T(8,128)(2,1)}, bf16[128,768]{1,0:T(8,128)(2,1)S(1)}, u32[]{:S(2)}, u32[]{:S(2)}) collective-permute-start(bf16[128,768]{1,0:T(8,128)(2,1)} %copy-done), channel_id=1, source_target_pairs={{0,16},{8,24},{16,0},{24,8},{32,48},{40,56},{48,32},{56,40},{64,80... | collective-permute-start | bytes 589832 | tf_op jit(solution)/shard_map/ppermute | solution.py:243
  28.3 7.7 %collective-permute-start.5 = (bf16[128,768]{1,0:T(8,128)(2,1)S(1)}, bf16[128,768]{1,0:T(8,128)(2,1)S(1)}, u32[]{:S(2)}, u32[]{:S(2)}) collective-permute-start(bf16[128,768]{1,0:T(8,128)(2,1)S(1)} %collective-permute-done.2.refs_7_), channel_id=1, source_target_pairs={{0,32},{8,40},{16,48},{24,56},{32,64},{40,72},{48,80},{56,88},{64,... | collective-permute-start | bytes 589832 | tf_op jit(solution)/shard_map/ppermute | solution.py:285
  28.8 7.3 %collective-permute-start.6 = (bf16[128,768]{1,0:T(8,128)(2,1)S(1)}, bf16[128,768]{1,0:T(8,128)(2,1)S(1)}, u32[]{:S(2)}, u32[]{:S(2)}) collective-permute-start(bf16[128,768]{1,0:T(8,128)(2,1)S(1)} %collective-permute-done.3.refs_8_), channel_id=1, source_target_pairs={{0,224},{8,232},{16,240},{24,248},{32,0},{40,8},{48,16},{56,24},{6... | collective-permute-start | bytes 589832 | tf_op jit(solution)/shard_map/ppermute | solution.py:286
  31.0 9.1 %collective-permute-start.10 = (bf16[128,768]{1,0:T(8,128)(2,1)}, bf16[128,768]{1,0:T(8,128)(2,1)S(1)}, u32[]{:S(2)}, u32[]{:S(2)}) collective-permute-start(bf16[128,768]{1,0:T(8,128)(2,1)} %copy-done), channel_id=1, source_target_pairs={{0,8},{8,0},{16,24},{24,16},{32,40},{40,32},{48,56},{56,48},{64,72... | collective-permute-start | bytes 589832 | tf_op jit(solution)/shard_map/ppermute | solution.py:244
  34.0 6.1 %collective-permute-start.12 = (bf16[128,768]{1,0:T(8,128)(2,1)S(1)}, bf16[128,768]{1,0:T(8,128)(2,1)S(1)}, u32[]{:S(2)}, u32[]{:S(2)}) collective-permute-start(bf16[128,768]{1,0:T(8,128)(2,1)S(1)} %collective-permute-done.11.refs_2_), channel_id=1, source_target_pairs={{0,8},{8,0},{16,24},{24,16},{32,40},{40,32},{48,56},{56,48},{64,72... | collective-permute-start | bytes 589832 | tf_op jit(solution)/shard_map/ppermute | solution.py:245
  36.1 4.8 %collective-permute-start.13 = (bf16[64,768]{1,0:T(8,128)(2,1)S(1)}, bf16[64,768]{1,0:T(8,128)(2,1)S(1)}, u32[]{:S(2)}, u32[]{:S(2)}) collective-permute-start(bf16[64,768]{1,0:T(8,128)(2,1)S(1)} %slice.45), channel_id=1, source_target_pairs={{0,32},{8,40},{16,48},{24,56},{32,64},{40,72},{48,80},{56,88},{64,... | collective-permute-start | bytes 294920 | tf_op jit(solution)/shard_map/ppermute | solution.py:288
  36.5 5.7 %collective-permute-start.14 = (bf16[64,768]{1,0:T(8,128)(2,1)S(1)}, bf16[64,768]{1,0:T(8,128)(2,1)S(1)}, u32[]{:S(2)}, u32[]{:S(2)}) collective-permute-start(bf16[64,768]{1,0:T(8,128)(2,1)S(1)} %slice.46), channel_id=1, source_target_pairs={{0,224},{8,232},{16,240},{24,248},{32,0},{40,8},{48,16},{56,24},{6... | collective-permute-start | bytes 294920 | tf_op jit(solution)/shard_map/ppermute | solution.py:289
  39.0 19.1 %collective-permute-start.8 = (bf16[128,768]{1,0:T(8,128)(2,1)S(1)}, bf16[128,768]{1,0:T(8,128)(2,1)S(1)}, u32[]{:S(2)}, u32[]{:S(2)}) collective-permute-start(bf16[128,768]{1,0:T(8,128)(2,1)S(1)} %constant_dynamic-update-slice_fusion.refs_4_.refs_0_), channel_id=1, source_target_pairs={{0,16},{8,24},{16,0},{24,8},{32,48},{40,56},{48,32},{56,40},{64,80... | collective-permute-start | bytes 589832 | tf_op jit(solution)/shard_map/ppermute | solution.py:243
  42.3 0.9 copy-start.1
  43.2 20.4 %copy-start.2 = (bf16[128,768]{1,0:T(8,128)(2,1)S(1)}, bf16[128,768]{1,0:T(8,128)(2,1)}, u32[]{:S(2)}) copy-start(bf16[128,768]{1,0:T(8,128)(2,1)} %copy-done) | copy-start | bytes 589828
  47.4 20.8 %all-to-all-start = ((f32[32,8,128]{2,1,0:T(8,128)}), f32[32,8,128]{2,1,0:T(8,128)S(1)}, u32[]{:S(2)}, u32[]{:S(2)}) async-start(f32[32,8,128]{2,1,0:T(8,128)} %get-tuple-element.33), calls=%async_computation | async-start | bytes 262144 | tf_op jit(solution)/shard_map/all_to_all | solution.py:308
  57.6 66.3 %all-gather.5.cloned.1.call-start = ((), (), s32[]{:S(2)}) async-start(), calls=%async_computation.2 | async-start | bytes 2654208 | tf_op jit(solution)/shard_map/all_gather | solution.py:347
  57.6 10.6 %collective-permute-start.7 = (bf16[128,768]{1,0:T(8,128)(2,1)S(1)}, bf16[128,768]{1,0:T(8,128)(2,1)S(1)}, u32[]{:S(2)}, u32[]{:S(2)}) collective-permute-start(bf16[128,768]{1,0:T(8,128)(2,1)S(1)} %constant_dynamic-update-slice_fusion.refs_4_.refs_0_), channel_id=1, source_target_pairs={{0,8},{8,0},{16,24},{24,16},{32,40},{40,32},{48,56},{56,48},{64,72... | collective-permute-start | bytes 589832 | tf_op jit(solution)/shard_map/ppermute | solution.py:244
  58.1 10.1 %collective-permute-start.9 = (bf16[128,768]{1,0:T(8,128)(2,1)S(1)}, bf16[128,768]{1,0:T(8,128)(2,1)S(1)}, u32[]{:S(2)}, u32[]{:S(2)}) collective-permute-start(bf16[128,768]{1,0:T(8,128)(2,1)S(1)} %collective-permute-done.8.refs_2_), channel_id=1, source_target_pairs={{0,8},{8,0},{16,24},{24,16},{32,40},{40,32},{48,56},{56,48},{64,72... | collective-permute-start | bytes 589832 | tf_op jit(solution)/shard_map/ppermute | solution.py:245
  58.2 2.1 %collective-permute-start.15 = (f32[8,512]{1,0:T(8,128)S(1)}, f32[8,512]{1,0:T(8,128)S(1)}, u32[]{:S(2)}, u32[]{:S(2)}) collective-permute-start(f32[8,512]{1,0:T(8,128)S(1)} %get-tuple-element.34.refs_13_), channel_id=1, source_target_pairs={{0,8},{8,0},{16,24},{24,16},{32,40},{40,32},{48,56},{56,48},{64,72... | collective-permute-start | bytes 49160 | tf_op jit(solution)/shard_map/ppermute | solution.py:316
  58.6 2.9 %collective-permute-start.16 = (f32[8,512]{1,0:T(8,128)S(1)}, f32[8,512]{1,0:T(8,128)S(1)}, u32[]{:S(2)}, u32[]{:S(2)}) collective-permute-start(f32[8,512]{1,0:T(8,128)S(1)} %get-tuple-element.34.refs_13_), channel_id=1, source_target_pairs={{0,16},{8,24},{16,0},{24,8},{32,48},{40,56},{48,32},{56,40},{64,80... | collective-permute-start | bytes 49160 | tf_op jit(solution)/shard_map/ppermute | solution.py:317
  60.0 3.6 %collective-permute-start.17 = (f32[8,512]{1,0:T(8,128)S(1)}, f32[8,512]{1,0:T(8,128)S(1)}, u32[]{:S(2)}, u32[]{:S(2)}) collective-permute-start(f32[8,512]{1,0:T(8,128)S(1)} %get-tuple-element.34.refs_13_), channel_id=1, source_target_pairs={{0,24},{8,16},{16,8},{24,0},{32,56},{40,48},{48,40},{56,32},{64,88... | collective-permute-start | bytes 49160 | tf_op jit(solution)/shard_map/ppermute | solution.py:318
  67.3 9.0 %collective-permute-start.24 = (bf16[2,128,384]{2,1,0:T(8,128)(2,1)}, bf16[2,128,384]{2,1,0:T(8,128)(2,1)S(1)}, u32[]{:S(2)}, u32[]{:S(2)}) collective-permute-start(bf16[2,128,384]{2,1,0:T(8,128)(2,1)} %get-tuple-element.35), channel_id=1, source_target_pairs={{0,8},{8,0},{16,24},{24,16},{32,40},{40,32},{48,56},{56,48},{64,72... | collective-permute-start | bytes 589832 | tf_op jit(solution)/shard_map/ppermute | solution.py:324
  68.2 1.4 copy-start.4
  73.8 4.0 %collective-permute-start.26 = (bf16[2,128,768]{2,1,0:T(8,128)(2,1)S(1)}, bf16[2,128,768]{2,1,0:T(8,128)(2,1)S(1)}, u32[]{:S(2)}, u32[]{:S(2)}) collective-permute-start(bf16[2,128,768]{2,1,0:T(8,128)(2,1)S(1)} %get-tuple-element.37), channel_id=1, source_target_pairs={{0,8},{8,0},{16,24},{24,16},{32,40},{40,32},{48,56},{56,48},{64,72... | collective-permute-start | bytes 1179656 | tf_op jit(solution)/shard_map/ppermute | solution.py:337
  76.4 4.5 %collective-permute-start.25 = (bf16[128,384]{1,0:T(8,128)(2,1)S(1)}, bf16[128,384]{1,0:T(8,128)(2,1)S(1)}, u32[]{:S(2)}, u32[]{:S(2)}) collective-permute-start(bf16[128,384]{1,0:T(8,128)(2,1)S(1)} %fusion.11), channel_id=1, source_target_pairs={{0,16},{8,24},{16,0},{24,8},{32,48},{40,56},{48,32},{56,40},{64,80... | collective-permute-start | bytes 294920 | tf_op jit(solution)/shard_map/ppermute | solution.py:343
  77.9 8.0 %copy-start.6 = (bf16[128,640]{1,0:T(8,128)(2,1)S(1)}, bf16[128,640]{1,0:T(8,128)(2,1)}, u32[]{:S(2)}) copy-start(bf16[128,640]{1,0:T(8,128)(2,1)} %copy-done.5) | copy-start | bytes 491524
  77.9 7.2 %collective-permute-start.27 = (bf16[128,768]{1,0:T(8,128)(2,1)S(1)}, bf16[128,768]{1,0:T(8,128)(2,1)S(1)}, u32[]{:S(2)}, u32[]{:S(2)}) collective-permute-start(bf16[128,768]{1,0:T(8,128)(2,1)S(1)} %fusion.6), channel_id=1, source_target_pairs={{0,16},{8,24},{16,0},{24,8},{32,48},{40,56},{48,32},{56,40},{64,80... | collective-permute-start | bytes 589832 | tf_op jit(solution)/shard_map/ppermute | solution.py:340
  85.9 0.7 collective-permute-start.18
  86.6 15.7 %collective-permute-start.19 = (bf16[128,640]{1,0:T(8,128)(2,1)S(1)}, bf16[128,640]{1,0:T(8,128)(2,1)S(1)}, u32[]{:S(2)}, u32[]{:S(2)}) collective-permute-start(bf16[128,640]{1,0:T(8,128)(2,1)S(1)} %collective-permute-done.18), channel_id=1, source_target_pairs={{0,4},{1,5},{2,6},{3,7},{4,0},{5,1},{6,2},{7,3},{8,12},{9,13},{10,... | collective-permute-start | bytes 491528 | tf_op jit(solution)/shard_map/ppermute | solution.py:349
  102.3 7.9 %collective-permute-start.20 = (bf16[256,640]{1,0:T(8,128)(2,1)S(1)}, bf16[256,640]{1,0:T(8,128)(2,1)S(1)}, u32[]{:S(2)}, u32[]{:S(2)}) collective-permute-start(bf16[256,640]{1,0:T(8,128)(2,1)S(1)} %constant_dynamic-update-slice_fusion.4.pair), channel_id=1, source_target_pairs={{0,1},{1,2},{2,3},{3,0},{4,5},{5,6},{6,7},{7,4},{8,9},{9,10},{10,1... | collective-permute-start | bytes 983048 | tf_op jit(solution)/shard_map/ppermute | solution.py:351
  103.9 6.9 %collective-permute-start.21 = (bf16[256,640]{1,0:T(8,128)(2,1)S(1)}, bf16[256,640]{1,0:T(8,128)(2,1)S(1)}, u32[]{:S(2)}, u32[]{:S(2)}) collective-permute-start(bf16[256,640]{1,0:T(8,128)(2,1)S(1)} %constant_dynamic-update-slice_fusion.4.pair), channel_id=1, source_target_pairs={{0,3},{1,0},{2,1},{3,2},{4,7},{5,4},{6,5},{7,6},{8,11},{9,8},{10,9... | collective-permute-start | bytes 983048 | tf_op jit(solution)/shard_map/ppermute | solution.py:352
  110.2 5.9 %collective-permute-start.22 = (bf16[128,640]{1,0:T(8,128)(2,1)S(1)}, bf16[128,640]{1,0:T(8,128)(2,1)S(1)}, u32[]{:S(2)}, u32[]{:S(2)}) collective-permute-start(bf16[128,640]{1,0:T(8,128)(2,1)S(1)} %slice.60), channel_id=1, source_target_pairs={{0,1},{1,2},{2,3},{3,0},{4,5},{5,6},{6,7},{7,4},{8,9},{9,10},{10,1... | collective-permute-start | bytes 491528 | tf_op jit(solution)/shard_map/ppermute | solution.py:360
  110.8 5.3 %collective-permute-start.23 = (bf16[128,640]{1,0:T(8,128)(2,1)S(1)}, bf16[128,640]{1,0:T(8,128)(2,1)S(1)}, u32[]{:S(2)}, u32[]{:S(2)}) collective-permute-start(bf16[128,640]{1,0:T(8,128)(2,1)S(1)} %slice.61), channel_id=1, source_target_pairs={{0,3},{1,0},{2,1},{3,2},{4,7},{5,4},{6,5},{7,6},{8,11},{9,8},{10,9... | collective-permute-start | bytes 491528 | tf_op jit(solution)/shard_map/ppermute | solution.py:361
  123.9 1.7 %copy-start.3 = (bf16[1024,1152]{1,0:T(8,128)(2,1)S(1)}, bf16[1024,1152]{1,0:T(8,128)(2,1)}, u32[]{:S(2)}) copy-start(bf16[1024,1152]{1,0:T(8,128)(2,1)} %all-gather.5.cloned.1.call-done.b) | copy-start | bytes 7077892
  128.8 5.8 %collective-permute-start.28 = (bf16[2,160,1152]{2,1,0:T(8,128)(2,1)}, bf16[2,160,1152]{2,1,0:T(8,128)(2,1)}, u32[]{:S(2)}, u32[]{:S(2)}) collective-permute-start(bf16[2,160,1152]{2,1,0:T(8,128)(2,1)} %get-tuple-element.42), channel_id=1, source_target_pairs={{0,8},{8,0},{16,24},{24,16},{32,40},{40,32},{48,56},{56,48},{64,72... | collective-permute-start | bytes 2211848 | tf_op jit(solution)/shard_map/ppermute | solution.py:250
  135.9 9.9 %collective-permute-start.29 = (bf16[160,1152]{1,0:T(8,128)(2,1)S(1)}, bf16[160,1152]{1,0:T(8,128)(2,1)S(1)}, u32[]{:S(2)}, u32[]{:S(2)}) collective-permute-start(bf16[160,1152]{1,0:T(8,128)(2,1)S(1)} %fusion.5), channel_id=1, source_target_pairs={{0,16},{8,24},{16,0},{24,8},{32,48},{40,56},{48,32},{56,40},{64,80... | collective-permute-start | bytes 1105928 | tf_op jit(solution)/shard_map/ppermute | solution.py:254
Sparse Core Ops, SparseCore 0:
  28.0 38.9 all-gather.2
  86.0 37.7 all-gather.4
where the time goes:
time: 154 us; the launch traced here: 153 us
  starting transfers between devices  66.2 us (43%)
  waiting for transfers between devices  45 us (29%)
  Pallas kernels  16.5 us (11%)
  between operations  14.2 us (9%)
  local copies, waits for them, and re-layouts  9.25 us (6%)
  other arithmetic  2.29 us (1%)
    pallas_call x5, Pallas kernels, call(): pl.pallas_call(kernel, out_shape=out_shape, in_specs=specs, out_specs=jax...  16.5 us
    ppermute x1, starting transfers between devices, shards(): moved_x = lax.ppermute(moved, 'tp', TP_X)  12.9 us
    all_to_all x1, starting transfers between devices, shards(): lax.all_to_all(stats_sent, 'ctx', split_axis=0, concat_axis=0, tiled=True)  10.1 us
    ppermute x1, waiting for transfers between devices, row_sum(): return mine + lax.ppermute(other, 'ctx', X_SWAP).astype(F32)  8.61 us
    all_gather x1, waiting for transfers between devices, shards(): lax.all_gather(grads, 'ctx', axis=0, tiled=True, axis_index_groups=Z_GROUPS)  6.76 us
    unnamed x17, local copies, waits for them, and re-layouts  5.83 us
    ppermute x1, waiting for transfers between devices, shards(): n_up = lax.ppermute(pair, 'tp', TP_UP)  4.76 us
    ppermute x1, waiting for transfers between devices, shards(): lax.ppermute(dkv_other, 'ctx', X_SWAP).astype(F32)  4.18 us
  transfers between devices with their start and end apart: 33, of which 15 were waited for; matrix products, arithmetic and copies ran while one was open for 2% of the time, Pallas kernels for 9%

commit v1 on v0

--- a/solution.py
+++ b/solution.py
@@ -74,13 +74,7 @@
     return [place[4 + 2 * lax.rem(z + s + PLANES, PLANES) + xl] for s in RING_SHIFT]
 
 
-def stats_kernel(place, *refs):
-    qg, kv_in, out, sent = refs[:4], refs[4:13], refs[13], refs[14]
-    qc, kc, sc = refs[15:]
-    fill(qc, qg)
-    fill(kc, kv_in)
-    q_row = lane_row(plane_tables(place))
-    k_st = ring_tables(place)
+def subset_stats(qc, kc, sc, q_row, k_st, out):
     out[...] = jnp.zeros_like(out)
     for h in range(HEADS_DEV):
         cols = slice(h * HD, (h + 1) * HD)
@@ -88,16 +82,16 @@
         qh = qc[:, cols]
         gh = qc[:, gcols]
         top = jnp.full((8, 4 * ROWS), LOW, F32)
-        for k in range(PLANES):
+        for k, stretch in enumerate(k_st):
             rows = slice(k * ROWS, (k + 1) * ROWS)
             s = dot(kc[rows, cols], qh, NT) * SCALE2
-            s = jnp.where(q_row >= k_st[k], s, LOW)
+            s = jnp.where(q_row >= stretch, s, LOW)
             sc[rows, :] = s
             top = jnp.maximum(top, fold(s, jnp.max))
         m = jnp.maximum(jnp.max(top, axis=0, keepdims=True), 0.1 * LOW)
         total = jnp.zeros((8, 4 * ROWS), F32)
         weighted = jnp.zeros((8, 4 * ROWS), F32)
-        for k in range(PLANES):
+        for k in range(len(k_st)):
             rows = slice(k * ROWS, (k + 1) * ROWS)
             dp = dot(kc[rows, gcols], gh, NT)
             e = jnp.exp2(sc[rows, :] - m)
@@ -108,6 +102,25 @@
         some = total > 0.0
         out[h : h + 1, :] = jnp.where(some, m + jnp.log2(total), 0.1 * LOW)
         out[3 + h : 4 + h, :] = jnp.where(some, weighted / total, 0.0)
+
+
+def near_stats_kernel(place, *refs):
+    qg, kv_in, out = refs[:4], refs[4:11], refs[11]
+    qc, kc, sc = refs[12:]
+    fill(qc, qg)
+    fill(kc, kv_in)
+    subset_stats(qc, kc, sc, lane_row(plane_tables(place)), ring_tables(place)[:7], out)
+
+
+def stats_kernel(place, *refs):
+    qg, kv_in, near, out, sent = refs[:4], refs[4:6], refs[6], refs[7], refs[8]
+    qc, kc, sc = refs[9:]
+    fill(qc, qg)
+    fill(kc, kv_in)
+    subset_stats(qc, kc, sc, lane_row(plane_tables(place)), ring_tables(place)[7:], out)
+    lse, delta = combine([near[...], out[...]])
+    out[0:3, :] = lse
+    out[3:6, :] = delta
     j = 2 * place[1] + place[2]
     for r in range(4):
         piece = out[:, r * ROWS : (r + 1) * ROWS]
@@ -116,10 +129,9 @@
 
 
 def combine(parts):
-    lse = [p[0:3] for p in parts]
-    top = jnp.maximum(jnp.maximum(lse[0], lse[1]), jnp.maximum(lse[2], lse[3]))
-    weights = [jnp.exp2(x - top) for x in lse]
-    total = weights[0] + weights[1] + weights[2] + weights[3]
+    top = functools.reduce(jnp.maximum, [p[0:3] for p in parts])
+    weights = [jnp.exp2(p[0:3] - top) for p in parts]
+    total = sum(weights)
     delta = sum(w * p[3:6] for w, p in zip(weights, parts))
     return top + jnp.log2(total), delta / total
 
@@ -163,9 +175,9 @@
                 send[r // 2, :, cols] = piece.astype(BF16)
 
 
-def dkey_kernel(place, *refs):
-    kv, qg, stats = refs[:4], refs[4], refs[5]
-    keep, send = refs[6:]
+def dkey_kernel(pieces, place, *refs):
+    count = len(pieces)
+    kv, qg, stats, outs = refs[:count], refs[count], refs[count + 1], refs[count + 2]
     z, xl = place[0], place[1]
     q_row = lane_row([place[4 + 2 * i + xl] for i in range(PLANES)])
     k_st = plane_tables(place)
@@ -179,19 +191,13 @@
         gh = qg[:, vcols]
         lse = all_lse[h : h + 1, :]
         delta = all_delta[h : h + 1, :]
-        for r in range(4):
-            s = dot(kv[r][:, cols], qh, NT) * SCALE2
+        for n, r in enumerate(pieces):
+            s = dot(kv[n][:, cols], qh, NT) * SCALE2
             p = jnp.where(q_row >= k_st[r], jnp.exp2(s - lse), 0.0)
-            dp = dot(kv[r][:, vcols], gh, NT)
+            dp = dot(kv[n][:, vcols], gh, NT)
             ds = (FACTOR * p * (dp - delta)).astype(BF16)
-            dv = dot(p.astype(BF16), gh, NN)
-            dk = dot(ds, qh, NN)
-            if r % 2 == 0:
-                keep[r // 2, :, cols] = dk
-                keep[r // 2, :, vcols] = dv
-            else:
-                send[r // 2, :, cols] = dk.astype(BF16)
-                send[r // 2, :, vcols] = dv.astype(BF16)
+            outs[n, :, cols] = dot(ds, qh, NN).astype(outs.dtype)
+            outs[n, :, vcols] = dot(p.astype(BF16), gh, NN).astype(outs.dtype)
 
 
 def normed_kernel(place, pair, up, down, up2, down2, out):
@@ -210,13 +216,16 @@
     put(down2[...], 1 - xh, y + 2)
 
 
-def product(place, at, b, keep, send):
+def product_kernel(place, at, rows, *outs):
     core = place[2]
-    for half in range(2):
-        mine = pl.multiple_of((2 * half + core) * 160, 160)
-        theirs = pl.multiple_of((2 * half + 1 - core) * 160, 160)
-        keep[half, :, :] = dot(at[pl.ds(mine, 160), :], b[...], NN)
-        send[half, :, :] = dot(at[pl.ds(theirs, 160), :], b[...], NN).astype(BF16)
+    for part in range(3):
+        keep, send = outs[2 * part], outs[2 * part + 1]
+        cols = slice(part * W, (part + 1) * W)
+        for half in range(2):
+            theirs = pl.multiple_of((2 * half + 1 - core) * 160, 160)
+            mine = pl.multiple_of((2 * half + core) * 160, 160)
+            send[half, :, :] = dot(at[pl.ds(theirs, 160), :], rows[:, cols], NN).astype(BF16)
+            keep[half, :, :] = dot(at[pl.ds(mine, 160), :], rows[:, cols], NN)
 
 
 def call(kernel, out_shape, *args, scratch=(), smem=0, flops=0, name=None):
@@ -229,7 +238,7 @@
         in_specs=specs,
         out_specs=jax.tree.map(lambda _: pl.BlockSpec(memory_space=pltpu.VMEM), out_shape),
         scratch_shapes=list(scratch),
-        compiler_params=pltpu.CompilerParams(vmem_limit_bytes=40 * 2**20),
+        compiler_params=pltpu.CompilerParams(vmem_limit_bytes=20 * 2**20),
         cost_estimate=pl.CostEstimate(flops=flops, bytes_accessed=size if flops else 0, transcendentals=0),
         name=name,
     )(*args)
@@ -288,21 +297,42 @@
     far_a = lax.ppermute(up3[:half], "ctx", Z_UP)
     far_b = lax.ppermute(down3[half:], "ctx", Z_DOWN)
     kv_plane = plane_gather(kv_later)
+    qg_plane[0] = jnp.concatenate([after(query_rows, up2), grad_output], axis=1)
     kv_ring = [kv_own, up1, down1, up2, down2, up3, down3, far_a, far_b]
 
     wide = [
         pltpu.VMEM((4 * ROWS, 2 * W), BF16),
         pltpu.VMEM((PLANES * ROWS, 2 * W), BF16),
     ]
+    near_stats = call(
+        near_stats_kernel,
+        shaped((8, 4 * ROWS), F32),
+        place,
+        *qg_plane,
+        *kv_ring[:7],
+        smem=1,
+        scratch=[
+            wide[0],
+            pltpu.VMEM((7 * ROWS, 2 * W), BF16),
+            pltpu.VMEM((7 * ROWS, 4 * ROWS), F32),
+        ],
+        flops=2 * 2 * 896 * 512 * W,
+        name="near_statistics",
+    )
     stats, stats_sent = call(
         stats_kernel,
         (shaped((8, 4 * ROWS), F32), shaped((CTX, 8, ROWS), F32)),
         place,
         *qg_plane,
-        *kv_ring,
+        *kv_ring[7:],
+        near_stats,
         smem=1,
-        scratch=wide + [pltpu.VMEM((PLANES * ROWS, 4 * ROWS), F32)],
-        flops=2 * 2 * 1024 * 512 * W,
+        scratch=[
+            wide[0],
+            pltpu.VMEM((ROWS, 2 * W), BF16),
+            pltpu.VMEM((ROWS, 4 * ROWS), F32),
+        ],
+        flops=2 * 2 * 128 * 512 * W,
         name="softmax_statistics",
     )
     all_stats = lax.all_to_all(stats_sent, "ctx", split_axis=0, concat_axis=0, tiled=True)
@@ -322,28 +352,34 @@
         name="query_gradient",
     )
     dq_got = lax.ppermute(dq_send, "ctx", CORE_SWAP).astype(F32)
+    def key_value_gradient(pieces, dtype, name):
+        return call(
+            functools.partial(dkey_kernel, pieces),
+            shaped((len(pieces), ROWS, 2 * W), dtype),
+            place,
+            *[kv_plane[r] for r in pieces],
+            qg_all,
+            all_stats,
+            smem=1,
+            flops=len(pieces) * 2 * 1024 * 512 * W,
+            name=name,
+        )
+
+    all_stats = after(all_stats, dq_send)
+    dkv_send = key_value_gradient((1, 3), BF16, "core_gradient")
+    all_stats = after(all_stats, dkv_send)
+    dkv_across = key_value_gradient((2,), F32, "across_gradient")
+    all_stats = after(all_stats, dkv_across)
+    dkv_own = key_value_gradient((0,), F32, "own_gradient")
     dq_other = (dq_keep[1] + dq_got[1]).astype(BF16)
-    dkv_keep, dkv_send = call(
-        dkey_kernel,
-        (shaped((2, ROWS, 2 * W), F32), shaped((2, ROWS, 2 * W), BF16)),
-        place,
-        *kv_plane,
-        qg_all,
-        after(all_stats, dq_send),
-        smem=1,
-        flops=4 * 2 * 1024 * 512 * W,
-        name="key_value_gradient",
-    )
+    dq_x = lax.ppermute(dq_other, "ctx", X_SWAP).astype(F32)
     dkv_got = lax.ppermute(dkv_send, "ctx", CORE_SWAP).astype(F32)
-    dkv_other = (dkv_keep[1] + dkv_got[1]).astype(BF16)
-    dkv = (
-        dkv_keep[0] + dkv_got[0] + lax.ppermute(dkv_other, "ctx", X_SWAP).astype(F32)
-    ).astype(BF16)
-    dq = (
-        dq_keep[0] + dq_got[0] + lax.ppermute(dq_other, "ctx", X_SWAP).astype(F32)
-    ).astype(BF16)
+    dkv_other = (dkv_across[0] + dkv_got[1]).astype(BF16)
+    dkv_x = lax.ppermute(dkv_other, "ctx", X_SWAP).astype(F32)
+    dq = dq_keep[0] + dq_got[0] + dq_x
+    dkv = dkv_own[0] + dkv_got[0] + dkv_x
+    grads = jnp.concatenate([dq, dkv], axis=1).astype(BF16)
     moved = lax.ppermute(after(turned_tp, dkv_send), ("ctx", "tp"), TURN_Z)
-    grads = jnp.concatenate([dq, dkv], axis=1)
     grads_all = lax.all_gather(grads, "ctx", axis=0, tiled=True, axis_index_groups=Z_GROUPS)
 
     moved_x = lax.ppermute(moved, "tp", TP_X)
@@ -362,9 +398,9 @@
         smem=1,
         name="normed_columns",
     )
-    keep, send = call(
-        product,
-        (shaped((2, 160, 3 * W), F32), shaped((2, 160, 3 * W), BF16)),
+    sums = call(
+        product_kernel,
+        (shaped((2, 160, W), F32), shaped((2, 160, W), BF16)) * 3,
         place,
         turned,
         grads_all,
@@ -372,8 +408,7 @@
         flops=2 * 640 * 1024 * 3 * W,
         name="weight_product",
     )
-    out = row_sum(keep, send, xl).astype(BF16)
-    return (out[:, :W], out[:, W : 2 * W], out[:, 2 * W :])
+    return tuple(row_sum(sums[2 * i], sums[2 * i + 1], xl).astype(BF16) for i in range(3))
 
 
 def solution(mesh):

time: 154 us -> 152 us (0.987)
  waiting for transfers between devices: 45 us -> 38.8 us
  Pallas kernels: 16.5 us -> 19.1 us
    ppermute x1 -> x3, waiting for transfers between devices: 8.61 us -> 5.45 us  [row_sum(): return mine + lax.ppermute(other, 'ctx', X_SWAP).astype(F32)]
    pallas_call x5 -> x8, Pallas kernels: 16.5 us -> 19.1 us  [call(): pl.pallas_call(kernel, out_shape=out_shape, in_specs=specs, out_specs=jax...]
    all_gather x1, waiting for transfers between devices: 0.01 us -> 2.08 us  [shards(): lax.all_gather(qg_sent, 'ctx', axis=0, tiled=True, axis_index_groups=Z_GR...]
    convert_element_type x4, other arithmetic: 0.2 us -> 2.06 us  [the longest x3 2.01 us: shards(): row_sum(sums[2 * i], sums[2 * i + 1], xl).astype(BF16)]
    ppermute x1, starting transfers between devices: 1.55 us -> 3.4 us  [shards(): n_down = lax.ppermute(pair, 'tp', TP_DOWN)]
    ppermute x2, waiting for transfers between devices: 5.88 us -> 4.07 us  [the longest x1 3.13 us: shards(): dkv_x = lax.ppermute(dkv_other, 'ctx', X_SWAP).astype(F32)]
    ppermute x1, starting transfers between devices: 2.49 us -> 4.2 us  [shards(): dkv_got = lax.ppermute(dkv_send, 'ctx', CORE_SWAP).astype(F32)]
    ppermute x1 -> x3, starting transfers between devices: 1.27 us -> 2.91 us  [row_sum(): return mine + lax.ppermute(other, 'ctx', X_SWAP).astype(F32)]
  transfers between devices with their start and end apart: 33 -> 37, of which waited for: 15 -> 17; matrix products, arithmetic and copies ran while one was open for 2% -> 4% of each run, Pallas kernels for 9% -> 10%
where the time goes in v1:
time: 152 us; the launch traced here: 151 us
  starting transfers between devices  67.1 us (44%)
  waiting for transfers between devices  38.8 us (26%)
  Pallas kernels  19.1 us (13%)
  between operations  14.4 us (9%)
  local copies, waits for them, and re-layouts  8.54 us (6%)
  other arithmetic  3.15 us (2%)
    pallas_call x8, Pallas kernels, call(): pl.pallas_call(kernel, out_shape=out_shape, in_specs=specs, out_specs=jax...  19.1 us
    ppermute x1, starting transfers between devices, shards(): moved_x = lax.ppermute(moved, 'tp', TP_X)  11.7 us
    all_to_all x1, starting transfers between devices, shards(): lax.all_to_all(stats_sent, 'ctx', split_axis=0, concat_axis=0, tiled=True)  9.29 us
    all_gather x1, waiting for transfers between devices, shards(): lax.all_gather(grads, 'ctx', axis=0, tiled=True, axis_index_groups=Z_GROUPS)  6.03 us
    unnamed x18, local copies, waits for them, and re-layouts  5.82 us
    ppermute x3, waiting for transfers between devices, row_sum(): return mine + lax.ppermute(other, 'ctx', X_SWAP).astype(F32)  5.45 us
    ppermute x1, waiting for transfers between devices, shards(): n_up = lax.ppermute(pair, 'tp', TP_UP)  5 us
    ppermute x1, starting transfers between devices, shards(): dkv_got = lax.ppermute(dkv_send, 'ctx', CORE_SWAP).astype(F32)  4.2 us
  transfers between devices with their start and end apart: 37, of which 17 were waited for; matrix products, arithmetic and copies ran while one was open for 4% of the time, Pallas kernels for 10%

profile of v1, /device:TPU:1, one launch (start us, length us, event | category | flops | bytes accessed | tf_op | source)
XLA Modules:
  0.0 151.1 jit_solution(11107784861621202571)
XLA Ops:
  7.2 0.9 constant_dynamic-update-slice_fusion.1
  8.1 0.9 constant_dynamic-update-slice_fusion.refs_4_.refs_0_
  9.0 2.5 %collective-permute-start = (bf16[128,768]{1,0:T(8,128)(2,1)S(1)}, bf16[128,768]{1,0:T(8,128)(2,1)S(1)}, u32[]{:S(2)}, u32[]{:S(2)}) collective-permute-start(bf16[128,768]{1,0:T(8,128)(2,1)S(1)} %constant_dynamic-update-slice_fusion.refs_4_.refs_0_), channel_id=1, source_target_pairs={{0,32},{8,40},{16,48},{24,56},{32,64},{40,72},{48,80},{56,88},{64,... | collective-permute-start | bytes 589832 | tf_op jit(solution)/shard_map/ppermute | solution.py:285
  11.6 4.0 %collective-permute-start.1 = (bf16[128,768]{1,0:T(8,128)(2,1)S(1)}, bf16[128,768]{1,0:T(8,128)(2,1)S(1)}, u32[]{:S(2)}, u32[]{:S(2)}) collective-permute-start(bf16[128,768]{1,0:T(8,128)(2,1)S(1)} %constant_dynamic-update-slice_fusion.refs_4_.refs_0_), channel_id=1, source_target_pairs={{0,224},{8,232},{16,240},{24,248},{32,0},{40,8},{48,16},{56,24},{6... | collective-permute-start | bytes 589832 | tf_op jit(solution)/shard_map/ppermute | solution.py:286
  15.6 1.6 %collective-permute-start.4 = (bf16[128,640]{1,0:T(8,128)(2,1)}, bf16[128,640]{1,0:T(8,128)(2,1)S(1)}, u32[]{:S(2)}, u32[]{:S(2)}) collective-permute-start(bf16[128,640]{1,0:T(8,128)(2,1)} %param.6), channel_id=1, source_target_pairs={{0,0},{1,1},{2,2},{3,3},{4,4},{5,5},{6,6},{7,7},{8,8},{9,9},{10,10... | collective-permute-start | bytes 491528 | tf_op jit(solution)/shard_map/ppermute | solution.py:288
  17.2 3.0 %collective-permute-done.refs_5_ = bf16[128,768]{1,0:T(8,128)(2,1)S(1)} collective-permute-done((bf16[128,768]{1,0:T(8,128)(2,1)S(1)}, bf16[128,768]{1,0:T(8,128)(2,1)S(1)}, u32[]{:S(2)}, u32[]{:S(2)}) %collective-permute-start) | collective-permute-done | bytes 196640 | tf_op jit(solution)/shard_map/ppermute | solution.py:285
  20.2 4.1 %collective-permute-start.3 = (bf16[128,768]{1,0:T(8,128)(2,1)S(1)}, bf16[128,768]{1,0:T(8,128)(2,1)S(1)}, u32[]{:S(2)}, u32[]{:S(2)}) collective-permute-start(bf16[128,768]{1,0:T(8,128)(2,1)S(1)} %collective-permute-done.1.refs_6_), channel_id=1, source_target_pairs={{0,224},{8,232},{16,240},{24,248},{32,0},{40,8},{48,16},{56,24},{6... | collective-permute-start | bytes 589832 | tf_op jit(solution)/shard_map/ppermute | solution.py:291
  24.3 0.9 constant_dynamic-update-slice_fusion.3
  25.2 0.9 constant_dynamic-update-slice_fusion.2
  26.1 1.8 %collective-permute-done.2.refs_7_ = bf16[128,768]{1,0:T(8,128)(2,1)S(1)} collective-permute-done((bf16[128,768]{1,0:T(8,128)(2,1)S(1)}, bf16[128,768]{1,0:T(8,128)(2,1)S(1)}, u32[]{:S(2)}, u32[]{:S(2)}) %collective-permute-start.2) | collective-permute-done | bytes 196640 | tf_op jit(solution)/shard_map/ppermute | solution.py:290
  28.8 2.2 %collective-permute-start.6 = (bf16[128,768]{1,0:T(8,128)(2,1)S(1)}, bf16[128,768]{1,0:T(8,128)(2,1)S(1)}, u32[]{:S(2)}, u32[]{:S(2)}) collective-permute-start(bf16[128,768]{1,0:T(8,128)(2,1)S(1)} %collective-permute-done.3.refs_8_), channel_id=1, source_target_pairs={{0,224},{8,232},{16,240},{24,248},{32,0},{40,8},{48,16},{56,24},{6... | collective-permute-start | bytes 589832 | tf_op jit(solution)/shard_map/ppermute | solution.py:295
  31.0 3.0 %collective-permute-start.10 = (bf16[128,768]{1,0:T(8,128)(2,1)}, bf16[128,768]{1,0:T(8,128)(2,1)S(1)}, u32[]{:S(2)}, u32[]{:S(2)}) collective-permute-start(bf16[128,768]{1,0:T(8,128)(2,1)} %copy-done.3), channel_id=1, source_target_pairs={{0,8},{8,0},{16,24},{24,16},{32,40},{40,32},{48,56},{56,48},{64,72... | collective-permute-start | bytes 589832 | tf_op jit(solution)/shard_map/ppermute | solution.py:253
  34.7 1.3 collective-permute-start.12
  36.0 0.9 constant_dynamic-update-slice_fusion.5
  37.5 2.5 %collective-permute-start.14 = (bf16[64,768]{1,0:T(8,128)(2,1)S(1)}, bf16[64,768]{1,0:T(8,128)(2,1)S(1)}, u32[]{:S(2)}, u32[]{:S(2)}) collective-permute-start(bf16[64,768]{1,0:T(8,128)(2,1)S(1)} %slice.31), channel_id=1, source_target_pairs={{0,224},{8,232},{16,240},{24,248},{32,0},{40,8},{48,16},{56,24},{6... | collective-permute-start | bytes 294920 | tf_op jit(solution)/shard_map/ppermute | solution.py:298
  40.3 2.8 %near_statistics.1.refs_6_ = f32[8,512]{1,0:T(8,128)S(1)} custom-call(s32[20]{0:T(128)S(1)} %concatenate.19.place, bf16[128,768]{1,0:T(8,128)(2,1)S(1)} %constant_dynamic-update-slice_fusion.4.refs_0_, bf16[128,768]{1,0:T(8,128)(2,1)S(1)} %collective-permute-done.10.refs_1_, bf16[128,768]{1,0:T(8,128)(2,1)S(1)} %collective-permute-done.11.refs_2_, ...), custom_call_target="tpu_custom_call" | custom-call | flops 704643072 | bytes 2162768 | tf_op jit(solution)/shard_map/near_statistics/pallas_call | solution.py:235
  43.1 1.8 %softmax_statistics.1 = (f32[8,512]{1,0:T(8,128)S(1)}, f32[32,8,128]{2,1,0:T(8,128)}) custom-call(s32[20]{0:T(128)S(1)} %concatenate.19.place, bf16[128,768]{1,0:T(8,128)(2,1)S(1)} %constant_dynamic-update-slice_fusion.4.refs_0_, bf16[128,768]{1,0:T(8,128)(2,1)S(1)} %collective-permute-done.10.refs_1_, bf16[128,768]{1,0:T(8,128)(2,1)S(1)} %collective-permute-done.11.refs_2_, ...), custom_call_target="tpu_custom_call" | custom-call | flops 100663296 | bytes 999504 | tf_op jit(solution)/shard_map/softmax_statistics/pallas_call | solution.py:235
  44.9 9.3 %all-to-all-start = ((f32[32,8,128]{2,1,0:T(8,128)}), f32[32,8,128]{2,1,0:T(8,128)S(1)}, u32[]{:S(2)}, u32[]{:S(2)}) async-start(f32[32,8,128]{2,1,0:T(8,128)} %get-tuple-element.39), calls=%async_computation | async-start | bytes 262144 | tf_op jit(solution)/shard_map/all_to_all | solution.py:338
  55.2 1.5 collective-permute-start.16
  57.2 1.1 collective-permute-done.16.refs_15_
  58.3 2.2 %collective-permute-done.17.refs_16_ = f32[8,512]{1,0:T(8,128)S(1)} collective-permute-done((f32[8,512]{1,0:T(8,128)S(1)}, f32[8,512]{1,0:T(8,128)S(1)}, u32[]{:S(2)}, u32[]{:S(2)}) %collective-permute-start.17) | collective-permute-done | bytes 16416 | tf_op jit(solution)/shard_map/ppermute | solution.py:348
  60.5 3.8 %query_gradient.1 = (f32[2,128,384]{2,1,0:T(8,128)S(1)}, bf16[2,128,384]{2,1,0:T(8,128)(2,1)}) custom-call(s32[20]{0:T(128)S(1)} %concatenate.19.place, bf16[128,768]{1,0:T(8,128)(2,1)S(1)} %constant_dynamic-update-slice_fusion.4.refs_0_, bf16[128,768]{1,0:T(8,128)(2,1)S(1)} %collective-permute-done.10.refs_1_, ...), custom_call_target="tpu_custom_call" | custom-call | tf_op jit(solution)/shard_map/query_gradient/pallas_call | solution.py:235
  64.8 2.1 %all-gather.3.cloned.1.call-done.refs_2_.refs_1_ = bf16[1024,768]{1,0:T(8,128)(2,1)} async-done(((bf16[128,768]{1,0:T(8,128)(2,1)}), bf16[1024,768]{1,0:T(8,128)(2,1)}) %all-gather.3.cloned.1.call-update) | async-done | bytes 1572880 | tf_op jit(solution)/shard_map/all_gather | solution.py:293
  66.9 1.4 copy-done
  68.3 2.8 %core_gradient.1 = bf16[2,128,768]{2,1,0:T(8,128)(2,1)S(1)} custom-call(s32[20]{0:T(128)S(1)} %concatenate.19.place, bf16[128,768]{1,0:T(8,128)(2,1)S(1)} %collective-permute-done.7.refs_0_, bf16[128,768]{1,0:T(8,128)(2,1)S(1)} %collective-permute-done.9.refs_1_, bf16[1024,768]{1,0:T(8,128)(2,1)S(1)} %copy-done, f32[32,8,128]{2,1,0:T(8,128)S(1)} %all-to-all-done.refs_3_.refs_2_), custom_call_target="tpu_custom_call" | custom-call | flops 805306368 | bytes 2097232 | tf_op jit(solution)/shard_map/core_gradient/pallas_call | solution.py:235
  71.2 4.2 %collective-permute-start.26 = (bf16[2,128,768]{2,1,0:T(8,128)(2,1)S(1)}, bf16[2,128,768]{2,1,0:T(8,128)(2,1)S(1)}, u32[]{:S(2)}, u32[]{:S(2)}) collective-permute-start(bf16[2,128,768]{2,1,0:T(8,128)(2,1)S(1)} %core_gradient.1), channel_id=1, source_target_pairs={{0,8},{8,0},{16,24},{24,16},{32,40},{40,32},{48,56},{56,48},{64,72... | collective-permute-start | bytes 1179656 | tf_op jit(solution)/shard_map/ppermute | solution.py:376
  75.4 1.3 collective-permute-start.25
  76.7 1.8 %across_gradient.1 = f32[1,128,768]{2,1,0:T(8,128)S(1)} custom-call(s32[20]{0:T(128)S(1)} %concatenate.19.place, bf16[128,768]{1,0:T(8,128)(2,1)S(1)} %collective-permute-done.8.refs_0_, bf16[1024,768]{1,0:T(8,128)(2,1)S(1)} %copy-done, f32[32,8,128]{2,1,0:T(8,128)S(1)} %all-to-all-done.refs_3_.refs_2_), custom_call_target="tpu_custom_call" | custom-call | flops 402653184 | bytes 1900624 | tf_op jit(solution)/shard_map/across_gradient/pallas_call | solution.py:235
  79.0 0.9 collective-permute-done.25
  80.0 1.8 %own_gradient.1 = f32[1,128,768]{2,1,0:T(8,128)S(1)} custom-call(s32[20]{0:T(128)S(1)} %concatenate.19.place, bf16[128,768]{1,0:T(8,128)(2,1)S(1)} %constant_dynamic-update-slice_fusion.refs_4_.refs_0_, bf16[1024,768]{1,0:T(8,128)(2,1)S(1)} %copy-done.1, f32[32,8,128]{2,1,0:T(8,128)S(1)} %all-to-all-done.refs_3_.refs_2_), custom_call_target="tpu_custom_call" | custom-call | flops 402653184 | bytes 1900624 | tf_op jit(solution)/shard_map/own_gradient/pallas_call | solution.py:235
  81.8 3.1 %collective-permute-done.27 = bf16[128,768]{1,0:T(8,128)(2,1)S(1)} collective-permute-done((bf16[128,768]{1,0:T(8,128)(2,1)S(1)}, bf16[128,768]{1,0:T(8,128)(2,1)S(1)}, u32[]{:S(2)}, u32[]{:S(2)}) %collective-permute-start.27) | collective-permute-done | bytes 196640 | tf_op jit(solution)/shard_map/ppermute | solution.py:378
  86.4 11.7 %collective-permute-start.19 = (bf16[128,640]{1,0:T(8,128)(2,1)S(1)}, bf16[128,640]{1,0:T(8,128)(2,1)S(1)}, u32[]{:S(2)}, u32[]{:S(2)}) collective-permute-start(bf16[128,640]{1,0:T(8,128)(2,1)S(1)} %collective-permute-done.18), channel_id=1, source_target_pairs={{0,4},{1,5},{2,6},{3,7},{4,0},{5,1},{6,2},{7,3},{8,12},{9,13},{10,... | collective-permute-start | bytes 491528 | tf_op jit(solution)/shard_map/ppermute | solution.py:385
  98.2 2.7 %collective-permute-done.19 = bf16[128,640]{1,0:T(8,128)(2,1)S(1)} collective-permute-done((bf16[128,640]{1,0:T(8,128)(2,1)S(1)}, bf16[128,640]{1,0:T(8,128)(2,1)S(1)}, u32[]{:S(2)}, u32[]{:S(2)}) %collective-permute-start.19) | collective-permute-done | bytes 163872 | tf_op jit(solution)/shard_map/ppermute | solution.py:385
  101.3 3.4 %collective-permute-start.21 = (bf16[256,640]{1,0:T(8,128)(2,1)S(1)}, bf16[256,640]{1,0:T(8,128)(2,1)S(1)}, u32[]{:S(2)}, u32[]{:S(2)}) collective-permute-start(bf16[256,640]{1,0:T(8,128)(2,1)S(1)} %constant_dynamic-update-slice_fusion.6.pair), channel_id=1, source_target_pairs={{0,3},{1,0},{2,1},{3,2},{4,7},{5,4},{6,5},{7,6},{8,11},{9,8},{10,9... | collective-permute-start | bytes 983048 | tf_op jit(solution)/shard_map/ppermute | solution.py:388
  104.7 5.0 %collective-permute-done.20.up = bf16[256,640]{1,0:T(8,128)(2,1)S(1)} collective-permute-done((bf16[256,640]{1,0:T(8,128)(2,1)S(1)}, bf16[256,640]{1,0:T(8,128)(2,1)S(1)}, u32[]{:S(2)}, u32[]{:S(2)}) %collective-permute-start.20) | collective-permute-done | bytes 327712 | tf_op jit(solution)/shard_map/ppermute | solution.py:387
  109.8 2.7 %collective-permute-start.23 = (bf16[128,640]{1,0:T(8,128)(2,1)S(1)}, bf16[128,640]{1,0:T(8,128)(2,1)S(1)}, u32[]{:S(2)}, u32[]{:S(2)}) collective-permute-start(bf16[128,640]{1,0:T(8,128)(2,1)S(1)} %slice.41), channel_id=1, source_target_pairs={{0,3},{1,0},{2,1},{3,2},{4,7},{5,4},{6,5},{7,6},{8,11},{9,8},{10,9... | collective-permute-start | bytes 491528 | tf_op jit(solution)/shard_map/ppermute | solution.py:397
  112.5 3.0 %collective-permute-done.22.up2 = bf16[128,640]{1,0:T(8,128)(2,1)S(1)} collective-permute-done((bf16[128,640]{1,0:T(8,128)(2,1)S(1)}, bf16[128,640]{1,0:T(8,128)(2,1)S(1)}, u32[]{:S(2)}, u32[]{:S(2)}) %collective-permute-start.22) | collective-permute-done | bytes 163872 | tf_op jit(solution)/shard_map/ppermute | solution.py:396
  116.3 1.0 normed_columns.1.at
  117.3 6.0 %all-gather.5.cloned.1.call-done.rows = bf16[1024,1152]{1,0:T(8,128)(2,1)} async-done(((bf16[128,1152]{1,0:T(8,128)(2,1)}), bf16[1024,1152]{1,0:T(8,128)(2,1)}) %all-gather.5.cloned.1.call-update) | async-done | bytes 2359312 | tf_op jit(solution)/shard_map/all_gather | solution.py:383
  123.3 1.7 %copy-done.2 = bf16[1024,1152]{1,0:T(8,128)(2,1)S(1)} copy-done((bf16[1024,1152]{1,0:T(8,128)(2,1)S(1)}, bf16[1024,1152]{1,0:T(8,128)(2,1)}, u32[]{:S(2)}) %copy-start.2) | copy-done | bytes 2359320
  125.0 3.3 %weight_product.1 = (f32[2,160,384]{2,1,0:T(8,128)S(1)}, bf16[2,160,384]{2,1,0:T(8,128)(2,1)S(1)}, f32[2,160,384]{2,1,0:T(8,128)S(1)}, bf16[2,160,384]{2,1,0:T(8...) custom-call(s32[20]{0:T(128)S(1)} %concatenate.19.place, ...), custom_call_target="tpu_custom_call" | custom-call | flops 1509949440 | bytes 3670096 | tf_op jit(solution)/shard_map/weight_product/pallas_call | solution.py:235
  128.3 3.6 %collective-permute-start.32 = (bf16[2,160,384]{2,1,0:T(8,128)(2,1)}, bf16[2,160,384]{2,1,0:T(8,128)(2,1)S(1)}, u32[]{:S(2)}, u32[]{:S(2)}) collective-permute-start(bf16[2,160,384]{2,1,0:T(8,128)(2,1)} %get-tuple-element.52), channel_id=1, source_target_pairs={{0,8},{8,0},{16,24},{24,16},{32,40},{40,32},{48,56},{56,48},{64,72... | collective-permute-start | bytes 737288 | tf_op jit(solution)/shard_map/ppermute | solution.py:259
  132.4 1.2 collective-permute-done.32
  133.7 1.3 collective-permute-start.33
  135.5 1.3 collective-permute-start.29
  136.8 1.5 %collective-permute-done.33 = bf16[160,384]{1,0:T(8,128)(2,1)S(1)} collective-permute-done((bf16[160,384]{1,0:T(8,128)(2,1)S(1)}, bf16[160,384]{1,0:T(8,128)(2,1)S(1)}, u32[]{:S(2)}, u32[]{:S(2)}) %collective-permute-start.33) | collective-permute-done | bytes 122912 | tf_op jit(solution)/shard_map/ppermute | solution.py:263
  139.0 2.0 %collective-permute-done.31 = bf16[160,384]{1,0:T(8,128)(2,1)S(1)} collective-permute-done((bf16[160,384]{1,0:T(8,128)(2,1)S(1)}, bf16[160,384]{1,0:T(8,128)(2,1)S(1)}, u32[]{:S(2)}, u32[]{:S(2)}) %collective-permute-start.31) | collective-permute-done | bytes 122912 | tf_op jit(solution)/shard_map/ppermute | solution.py:263
  141.6 2.0 %collective-permute-done.29 = bf16[160,384]{1,0:T(8,128)(2,1)S(1)} collective-permute-done((bf16[160,384]{1,0:T(8,128)(2,1)S(1)}, bf16[160,384]{1,0:T(8,128)(2,1)S(1)}, u32[]{:S(2)}, u32[]{:S(2)}) %collective-permute-start.29) | collective-permute-done | bytes 122912 | tf_op jit(solution)/shard_map/ppermute | solution.py:263
  (79 shorter events, 10.9 us)
Async XLA Ops:
  7.2 33.1 %copy-start.4 = (bf16[128,384]{1,0:T(8,128)(2,1)S(1)}, bf16[128,384]{1,0:T(8,128)(2,1)}, u32[]{:S(2)}) copy-start(bf16[128,384]{1,0:T(8,128)(2,1)} %param.10) | copy-start | bytes 294916
  7.2 59.7 %all-gather.3.cloned.1.call-start = ((), (), s32[]{:S(2)}) async-start(), calls=%async_computation.1 | async-start | bytes 1769472 | tf_op jit(solution)/shard_map/all_gather | solution.py:293
  9.0 11.1 %collective-permute-start = (bf16[128,768]{1,0:T(8,128)(2,1)S(1)}, bf16[128,768]{1,0:T(8,128)(2,1)S(1)}, u32[]{:S(2)}, u32[]{:S(2)}) collective-permute-start(bf16[128,768]{1,0:T(8,128)(2,1)S(1)} %constant_dynamic-update-slice_fusion.refs_4_.refs_0_), channel_id=1, source_target_pairs={{0,32},{8,40},{16,48},{24,56},{32,64},{40,72},{48,80},{56,88},{64,... | collective-permute-start | bytes 589832 | tf_op jit(solution)/shard_map/ppermute | solution.py:285
  11.6 8.6 %collective-permute-start.1 = (bf16[128,768]{1,0:T(8,128)(2,1)S(1)}, bf16[128,768]{1,0:T(8,128)(2,1)S(1)}, u32[]{:S(2)}, u32[]{:S(2)}) collective-permute-start(bf16[128,768]{1,0:T(8,128)(2,1)S(1)} %constant_dynamic-update-slice_fusion.refs_4_.refs_0_), channel_id=1, source_target_pairs={{0,224},{8,232},{16,240},{24,248},{32,0},{40,8},{48,16},{56,24},{6... | collective-permute-start | bytes 589832 | tf_op jit(solution)/shard_map/ppermute | solution.py:286
  15.6 10.5 %collective-permute-start.4 = (bf16[128,640]{1,0:T(8,128)(2,1)}, bf16[128,640]{1,0:T(8,128)(2,1)S(1)}, u32[]{:S(2)}, u32[]{:S(2)}) collective-permute-start(bf16[128,640]{1,0:T(8,128)(2,1)} %param.6), channel_id=1, source_target_pairs={{0,0},{1,1},{2,2},{3,3},{4,4},{5,5},{6,6},{7,7},{8,8},{9,9},{10,10... | collective-permute-start | bytes 491528 | tf_op jit(solution)/shard_map/ppermute | solution.py:288
  20.2 7.7 %collective-permute-start.2 = (bf16[128,768]{1,0:T(8,128)(2,1)S(1)}, bf16[128,768]{1,0:T(8,128)(2,1)S(1)}, u32[]{:S(2)}, u32[]{:S(2)}) collective-permute-start(bf16[128,768]{1,0:T(8,128)(2,1)S(1)} %collective-permute-done.refs_5_), channel_id=1, source_target_pairs={{0,32},{8,40},{16,48},{24,56},{32,64},{40,72},{48,80},{56,88},{64,... | collective-permute-start | bytes 589832 | tf_op jit(solution)/shard_map/ppermute | solution.py:290
  20.2 7.7 %collective-permute-start.3 = (bf16[128,768]{1,0:T(8,128)(2,1)S(1)}, bf16[128,768]{1,0:T(8,128)(2,1)S(1)}, u32[]{:S(2)}, u32[]{:S(2)}) collective-permute-start(bf16[128,768]{1,0:T(8,128)(2,1)S(1)} %collective-permute-done.1.refs_6_), channel_id=1, source_target_pairs={{0,224},{8,232},{16,240},{24,248},{32,0},{40,8},{48,16},{56,24},{6... | collective-permute-start | bytes 589832 | tf_op jit(solution)/shard_map/ppermute | solution.py:291
  26.1 1.8 %copy-start.3 = (bf16[128,768]{1,0:T(8,128)(2,1)}, bf16[128,768]{1,0:T(8,128)(2,1)S(1)}, u32[]{:S(2)}) copy-start(bf16[128,768]{1,0:T(8,128)(2,1)S(1)} %constant_dynamic-update-slice_fusion.2) | copy-start | bytes 589828
  26.1 8.6 %copy-start.5 = (bf16[128,640]{1,0:T(8,128)(2,1)}, bf16[128,640]{1,0:T(8,128)(2,1)S(1)}, u32[]{:S(2)}) copy-start(bf16[128,640]{1,0:T(8,128)(2,1)S(1)} %collective-permute-done.4) | copy-start | bytes 491524
  27.9 6.8 %collective-permute-start.11 = (bf16[128,768]{1,0:T(8,128)(2,1)}, bf16[128,768]{1,0:T(8,128)(2,1)S(1)}, u32[]{:S(2)}, u32[]{:S(2)}) collective-permute-start(bf16[128,768]{1,0:T(8,128)(2,1)} %copy-done.3), channel_id=1, source_target_pairs={{0,16},{8,24},{16,0},{24,8},{32,48},{40,56},{48,32},{56,40},{64,80... | collective-permute-start | bytes 589832 | tf_op jit(solution)/shard_map/ppermute | solution.py:252
  28.3 8.6 %collective-permute-start.5 = (bf16[128,768]{1,0:T(8,128)(2,1)S(1)}, bf16[128,768]{1,0:T(8,128)(2,1)S(1)}, u32[]{:S(2)}, u32[]{:S(2)}) collective-permute-start(bf16[128,768]{1,0:T(8,128)(2,1)S(1)} %collective-permute-done.2.refs_7_), channel_id=1, source_target_pairs={{0,32},{8,40},{16,48},{24,56},{32,64},{40,72},{48,80},{56,88},{64,... | collective-permute-start | bytes 589832 | tf_op jit(solution)/shard_map/ppermute | solution.py:294
  28.8 8.2 %collective-permute-start.6 = (bf16[128,768]{1,0:T(8,128)(2,1)S(1)}, bf16[128,768]{1,0:T(8,128)(2,1)S(1)}, u32[]{:S(2)}, u32[]{:S(2)}) collective-permute-start(bf16[128,768]{1,0:T(8,128)(2,1)S(1)} %collective-permute-done.3.refs_8_), channel_id=1, source_target_pairs={{0,224},{8,232},{16,240},{24,248},{32,0},{40,8},{48,16},{56,24},{6... | collective-permute-start | bytes 589832 | tf_op jit(solution)/shard_map/ppermute | solution.py:295
  31.0 9.3 %collective-permute-start.10 = (bf16[128,768]{1,0:T(8,128)(2,1)}, bf16[128,768]{1,0:T(8,128)(2,1)S(1)}, u32[]{:S(2)}, u32[]{:S(2)}) collective-permute-start(bf16[128,768]{1,0:T(8,128)(2,1)} %copy-done.3), channel_id=1, source_target_pairs={{0,8},{8,0},{16,24},{24,16},{32,40},{40,32},{48,56},{56,48},{64,72... | collective-permute-start | bytes 589832 | tf_op jit(solution)/shard_map/ppermute | solution.py:253
  34.7 5.5 %collective-permute-start.12 = (bf16[128,768]{1,0:T(8,128)(2,1)S(1)}, bf16[128,768]{1,0:T(8,128)(2,1)S(1)}, u32[]{:S(2)}, u32[]{:S(2)}) collective-permute-start(bf16[128,768]{1,0:T(8,128)(2,1)S(1)} %collective-permute-done.11.refs_2_), channel_id=1, source_target_pairs={{0,8},{8,0},{16,24},{24,16},{32,40},{40,32},{48,56},{56,48},{64,72... | collective-permute-start | bytes 589832 | tf_op jit(solution)/shard_map/ppermute | solution.py:254
  37.0 6.1 %collective-permute-start.13 = (bf16[64,768]{1,0:T(8,128)(2,1)S(1)}, bf16[64,768]{1,0:T(8,128)(2,1)S(1)}, u32[]{:S(2)}, u32[]{:S(2)}) collective-permute-start(bf16[64,768]{1,0:T(8,128)(2,1)S(1)} %slice.30), channel_id=1, source_target_pairs={{0,32},{8,40},{16,48},{24,56},{32,64},{40,72},{48,80},{56,88},{64,... | collective-permute-start | bytes 294920 | tf_op jit(solution)/shard_map/ppermute | solution.py:297
  37.5 5.6 %collective-permute-start.14 = (bf16[64,768]{1,0:T(8,128)(2,1)S(1)}, bf16[64,768]{1,0:T(8,128)(2,1)S(1)}, u32[]{:S(2)}, u32[]{:S(2)}) collective-permute-start(bf16[64,768]{1,0:T(8,128)(2,1)S(1)} %slice.31), channel_id=1, source_target_pairs={{0,224},{8,232},{16,240},{24,248},{32,0},{40,8},{48,16},{56,24},{6... | collective-permute-start | bytes 294920 | tf_op jit(solution)/shard_map/ppermute | solution.py:298
  39.9 14.8 %collective-permute-start.8 = (bf16[128,768]{1,0:T(8,128)(2,1)S(1)}, bf16[128,768]{1,0:T(8,128)(2,1)S(1)}, u32[]{:S(2)}, u32[]{:S(2)}) collective-permute-start(bf16[128,768]{1,0:T(8,128)(2,1)S(1)} %constant_dynamic-update-slice_fusion.refs_4_.refs_0_), channel_id=1, source_target_pairs={{0,16},{8,24},{16,0},{24,8},{32,48},{40,56},{48,32},{56,40},{64,80... | collective-permute-start | bytes 589832 | tf_op jit(solution)/shard_map/ppermute | solution.py:252
  44.9 19.9 %all-to-all-start = ((f32[32,8,128]{2,1,0:T(8,128)}), f32[32,8,128]{2,1,0:T(8,128)S(1)}, u32[]{:S(2)}, u32[]{:S(2)}) async-start(f32[32,8,128]{2,1,0:T(8,128)} %get-tuple-element.39), calls=%async_computation | async-start | bytes 262144 | tf_op jit(solution)/shard_map/all_to_all | solution.py:338
  54.2 69.1 %all-gather.5.cloned.1.call-start = ((), (), s32[]{:S(2)}) async-start(), calls=%async_computation.2 | async-start | bytes 2654208 | tf_op jit(solution)/shard_map/all_gather | solution.py:383
  54.2 10.6 %collective-permute-start.7 = (bf16[128,768]{1,0:T(8,128)(2,1)S(1)}, bf16[128,768]{1,0:T(8,128)(2,1)S(1)}, u32[]{:S(2)}, u32[]{:S(2)}) collective-permute-start(bf16[128,768]{1,0:T(8,128)(2,1)S(1)} %constant_dynamic-update-slice_fusion.refs_4_.refs_0_), channel_id=1, source_target_pairs={{0,8},{8,0},{16,24},{24,16},{32,40},{40,32},{48,56},{56,48},{64,72... | collective-permute-start | bytes 589832 | tf_op jit(solution)/shard_map/ppermute | solution.py:253
  54.7 10.1 %collective-permute-start.9 = (bf16[128,768]{1,0:T(8,128)(2,1)S(1)}, bf16[128,768]{1,0:T(8,128)(2,1)S(1)}, u32[]{:S(2)}, u32[]{:S(2)}) collective-permute-start(bf16[128,768]{1,0:T(8,128)(2,1)S(1)} %collective-permute-done.8.refs_0_), channel_id=1, source_target_pairs={{0,8},{8,0},{16,24},{24,16},{32,40},{40,32},{48,56},{56,48},{64,72... | collective-permute-start | bytes 589832 | tf_op jit(solution)/shard_map/ppermute | solution.py:254
  55.0 2.1 %collective-permute-start.15 = (f32[8,512]{1,0:T(8,128)S(1)}, f32[8,512]{1,0:T(8,128)S(1)}, u32[]{:S(2)}, u32[]{:S(2)}) collective-permute-start(f32[8,512]{1,0:T(8,128)S(1)} %get-tuple-element.40.refs_13_), channel_id=1, source_target_pairs={{0,8},{8,0},{16,24},{24,16},{32,40},{40,32},{48,56},{56,48},{64,72... | collective-permute-start | bytes 49160 | tf_op jit(solution)/shard_map/ppermute | solution.py:346
  55.2 3.0 %collective-permute-start.16 = (f32[8,512]{1,0:T(8,128)S(1)}, f32[8,512]{1,0:T(8,128)S(1)}, u32[]{:S(2)}, u32[]{:S(2)}) collective-permute-start(f32[8,512]{1,0:T(8,128)S(1)} %get-tuple-element.40.refs_13_), channel_id=1, source_target_pairs={{0,16},{8,24},{16,0},{24,8},{32,48},{40,56},{48,32},{56,40},{64,80... | collective-permute-start | bytes 49160 | tf_op jit(solution)/shard_map/ppermute | solution.py:347
  56.8 3.8 %collective-permute-start.17 = (f32[8,512]{1,0:T(8,128)S(1)}, f32[8,512]{1,0:T(8,128)S(1)}, u32[]{:S(2)}, u32[]{:S(2)}) collective-permute-start(f32[8,512]{1,0:T(8,128)S(1)} %get-tuple-element.40.refs_13_), channel_id=1, source_target_pairs={{0,24},{8,16},{16,8},{24,0},{32,56},{40,48},{48,40},{56,32},{64,88... | collective-permute-start | bytes 49160 | tf_op jit(solution)/shard_map/ppermute | solution.py:348
  64.3 11.1 %collective-permute-start.24 = (bf16[2,128,384]{2,1,0:T(8,128)(2,1)}, bf16[2,128,384]{2,1,0:T(8,128)(2,1)S(1)}, u32[]{:S(2)}, u32[]{:S(2)}) collective-permute-start(bf16[2,128,384]{2,1,0:T(8,128)(2,1)} %get-tuple-element.41), channel_id=1, source_target_pairs={{0,8},{8,0},{16,24},{24,16},{32,40},{40,32},{48,56},{56,48},{64,72... | collective-permute-start | bytes 589832 | tf_op jit(solution)/shard_map/ppermute | solution.py:354
  66.9 1.4 copy-start
  71.2 7.3 %collective-permute-start.26 = (bf16[2,128,768]{2,1,0:T(8,128)(2,1)S(1)}, bf16[2,128,768]{2,1,0:T(8,128)(2,1)S(1)}, u32[]{:S(2)}, u32[]{:S(2)}) collective-permute-start(bf16[2,128,768]{2,1,0:T(8,128)(2,1)S(1)} %core_gradient.1), channel_id=1, source_target_pairs={{0,8},{8,0},{16,24},{24,16},{32,40},{40,32},{48,56},{56,48},{64,72... | collective-permute-start | bytes 1179656 | tf_op jit(solution)/shard_map/ppermute | solution.py:376
  75.4 4.5 %collective-permute-start.25 = (bf16[128,384]{1,0:T(8,128)(2,1)S(1)}, bf16[128,384]{1,0:T(8,128)(2,1)S(1)}, u32[]{:S(2)}, u32[]{:S(2)}) collective-permute-start(bf16[128,384]{1,0:T(8,128)(2,1)S(1)} %fusion.15), channel_id=1, source_target_pairs={{0,16},{8,24},{16,0},{24,8},{32,48},{40,56},{48,32},{56,40},{64,80... | collective-permute-start | bytes 294920 | tf_op jit(solution)/shard_map/ppermute | solution.py:375
  78.5 1.5 copy-start.1
  78.6 6.3 %collective-permute-start.27 = (bf16[128,768]{1,0:T(8,128)(2,1)S(1)}, bf16[128,768]{1,0:T(8,128)(2,1)S(1)}, u32[]{:S(2)}, u32[]{:S(2)}) collective-permute-start(bf16[128,768]{1,0:T(8,128)(2,1)S(1)} %fusion.7), channel_id=1, source_target_pairs={{0,16},{8,24},{16,0},{24,8},{32,48},{40,56},{48,32},{56,40},{64,80... | collective-permute-start | bytes 589832 | tf_op jit(solution)/shard_map/ppermute | solution.py:378
  81.8 4.0 %copy-start.6 = (bf16[128,640]{1,0:T(8,128)(2,1)S(1)}, bf16[128,640]{1,0:T(8,128)(2,1)}, u32[]{:S(2)}) copy-start(bf16[128,640]{1,0:T(8,128)(2,1)} %copy-done.5) | copy-start | bytes 491524
  85.7 0.7 collective-permute-start.18
  86.4 14.4 %collective-permute-start.19 = (bf16[128,640]{1,0:T(8,128)(2,1)S(1)}, bf16[128,640]{1,0:T(8,128)(2,1)S(1)}, u32[]{:S(2)}, u32[]{:S(2)}) collective-permute-start(bf16[128,640]{1,0:T(8,128)(2,1)S(1)} %collective-permute-done.18), channel_id=1, source_target_pairs={{0,4},{1,5},{2,6},{3,7},{4,0},{5,1},{6,2},{7,3},{8,12},{9,13},{10,... | collective-permute-start | bytes 491528 | tf_op jit(solution)/shard_map/ppermute | solution.py:385
  100.9 8.8 %collective-permute-start.20 = (bf16[256,640]{1,0:T(8,128)(2,1)S(1)}, bf16[256,640]{1,0:T(8,128)(2,1)S(1)}, u32[]{:S(2)}, u32[]{:S(2)}) collective-permute-start(bf16[256,640]{1,0:T(8,128)(2,1)S(1)} %constant_dynamic-update-slice_fusion.6.pair), channel_id=1, source_target_pairs={{0,1},{1,2},{2,3},{3,0},{4,5},{5,6},{6,7},{7,4},{8,9},{9,10},{10,1... | collective-permute-start | bytes 983048 | tf_op jit(solution)/shard_map/ppermute | solution.py:387
  101.3 8.5 %collective-permute-start.21 = (bf16[256,640]{1,0:T(8,128)(2,1)S(1)}, bf16[256,640]{1,0:T(8,128)(2,1)S(1)}, u32[]{:S(2)}, u32[]{:S(2)}) collective-permute-start(bf16[256,640]{1,0:T(8,128)(2,1)S(1)} %constant_dynamic-update-slice_fusion.6.pair), channel_id=1, source_target_pairs={{0,3},{1,0},{2,1},{3,2},{4,7},{5,4},{6,5},{7,6},{8,11},{9,8},{10,9... | collective-permute-start | bytes 983048 | tf_op jit(solution)/shard_map/ppermute | solution.py:388
  109.7 5.9 %collective-permute-start.22 = (bf16[128,640]{1,0:T(8,128)(2,1)S(1)}, bf16[128,640]{1,0:T(8,128)(2,1)S(1)}, u32[]{:S(2)}, u32[]{:S(2)}) collective-permute-start(bf16[128,640]{1,0:T(8,128)(2,1)S(1)} %slice.40), channel_id=1, source_target_pairs={{0,1},{1,2},{2,3},{3,0},{4,5},{5,6},{6,7},{7,4},{8,9},{9,10},{10,1... | collective-permute-start | bytes 491528 | tf_op jit(solution)/shard_map/ppermute | solution.py:396
  109.8 6.5 %collective-permute-start.23 = (bf16[128,640]{1,0:T(8,128)(2,1)S(1)}, bf16[128,640]{1,0:T(8,128)(2,1)S(1)}, u32[]{:S(2)}, u32[]{:S(2)}) collective-permute-start(bf16[128,640]{1,0:T(8,128)(2,1)S(1)} %slice.41), channel_id=1, source_target_pairs={{0,3},{1,0},{2,1},{3,2},{4,7},{5,4},{6,5},{7,6},{8,11},{9,8},{10,9... | collective-permute-start | bytes 491528 | tf_op jit(solution)/shard_map/ppermute | solution.py:397
  123.3 1.7 %copy-start.2 = (bf16[1024,1152]{1,0:T(8,128)(2,1)S(1)}, bf16[1024,1152]{1,0:T(8,128)(2,1)}, u32[]{:S(2)}) copy-start(bf16[1024,1152]{1,0:T(8,128)(2,1)} %all-gather.5.cloned.1.call-done.rows) | copy-start | bytes 7077892
  128.3 5.3 %collective-permute-start.32 = (bf16[2,160,384]{2,1,0:T(8,128)(2,1)}, bf16[2,160,384]{2,1,0:T(8,128)(2,1)S(1)}, u32[]{:S(2)}, u32[]{:S(2)}) collective-permute-start(bf16[2,160,384]{2,1,0:T(8,128)(2,1)} %get-tuple-element.52), channel_id=1, source_target_pairs={{0,8},{8,0},{16,24},{24,16},{32,40},{40,32},{48,56},{56,48},{64,72... | collective-permute-start | bytes 737288 | tf_op jit(solution)/shard_map/ppermute | solution.py:259
  131.9 3.0 %collective-permute-start.30 = (bf16[2,160,384]{2,1,0:T(8,128)(2,1)S(1)}, bf16[2,160,384]{2,1,0:T(8,128)(2,1)S(1)}, u32[]{:S(2)}, u32[]{:S(2)}) collective-permute-start(bf16[2,160,384]{2,1,0:T(8,128)(2,1)S(1)} %get-tuple-element.50), channel_id=1, source_target_pairs={{0,8},{8,0},{16,24},{24,16},{32,40},{40,32},{48,56},{56,48},{64,72... | collective-permute-start | bytes 737288 | tf_op jit(solution)/shard_map/ppermute | solution.py:259
  131.9 3.5 %collective-permute-start.28 = (bf16[2,160,384]{2,1,0:T(8,128)(2,1)S(1)}, bf16[2,160,384]{2,1,0:T(8,128)(2,1)S(1)}, u32[]{:S(2)}, u32[]{:S(2)}) collective-permute-start(bf16[2,160,384]{2,1,0:T(8,128)(2,1)S(1)} %get-tuple-element.48), channel_id=1, source_target_pairs={{0,8},{8,0},{16,24},{24,16},{32,40},{40,32},{48,56},{56,48},{64,72... | collective-permute-start | bytes 737288 | tf_op jit(solution)/shard_map/ppermute | solution.py:259
  133.7 4.6 %collective-permute-start.33 = (bf16[160,384]{1,0:T(8,128)(2,1)S(1)}, bf16[160,384]{1,0:T(8,128)(2,1)S(1)}, u32[]{:S(2)}, u32[]{:S(2)}) collective-permute-start(bf16[160,384]{1,0:T(8,128)(2,1)S(1)} %fusion.14), channel_id=1, source_target_pairs={{0,16},{8,24},{16,0},{24,8},{32,48},{40,56},{48,32},{56,40},{64,80... | collective-permute-start | bytes 368648 | tf_op jit(solution)/shard_map/ppermute | solution.py:263
  135.0 5.9 %collective-permute-start.31 = (bf16[160,384]{1,0:T(8,128)(2,1)S(1)}, bf16[160,384]{1,0:T(8,128)(2,1)S(1)}, u32[]{:S(2)}, u32[]{:S(2)}) collective-permute-start(bf16[160,384]{1,0:T(8,128)(2,1)S(1)} %fusion.13), channel_id=1, source_target_pairs={{0,16},{8,24},{16,0},{24,8},{32,48},{40,56},{48,32},{56,40},{64,80... | collective-permute-start | bytes 368648 | tf_op jit(solution)/shard_map/ppermute | solution.py:263
  135.5 8.1 %collective-permute-start.29 = (bf16[160,384]{1,0:T(8,128)(2,1)S(1)}, bf16[160,384]{1,0:T(8,128)(2,1)S(1)}, u32[]{:S(2)}, u32[]{:S(2)}) collective-permute-start(bf16[160,384]{1,0:T(8,128)(2,1)S(1)} %fusion.12), channel_id=1, source_target_pairs={{0,16},{8,24},{16,0},{24,8},{32,48},{40,56},{48,32},{56,40},{64,80... | collective-permute-start | bytes 368648 | tf_op jit(solution)/shard_map/ppermute | solution.py:263
Sparse Core Ops, SparseCore 0:
  28.0 38.8 all-gather.2
  85.8 37.4 all-gather.4

commit v2 on v1

--- a/solution.py
+++ b/solution.py
@@ -286,14 +286,16 @@
     down1 = lax.ppermute(kv_own, "ctx", Z_DOWN)
     qg_plane = plane_gather(qg_own)
     turned_tp = lax.ppermute(normed_rows, ("ctx", "tp"), TURN_TP)
-    up1, down1 = lax.optimization_barrier((up1, down1))
+    up1, down1, qg_sent, turned_tp = lax.optimization_barrier(
+        (up1, down1, qg_own, turned_tp)
+    )
+    qg_all = lax.all_gather(qg_sent, "ctx", axis=0, tiled=True, axis_index_groups=Z_GROUPS)
     up2 = lax.ppermute(up1, "ctx", Z_UP)
     down2 = lax.ppermute(down1, "ctx", Z_DOWN)
-    up2, down2, qg_sent, turned_tp = lax.optimization_barrier((up2, down2, qg_own, turned_tp))
-    qg_all = lax.all_gather(qg_sent, "ctx", axis=0, tiled=True, axis_index_groups=Z_GROUPS)
+    up2, down2 = lax.optimization_barrier((up2, down2))
     up3 = lax.ppermute(up2, "ctx", Z_UP)
     down3 = lax.ppermute(down2, "ctx", Z_DOWN)
-    up3, down3, kv_later, turned_tp = lax.optimization_barrier((up3, down3, kv_own, turned_tp))
+    up3, down3, kv_later = lax.optimization_barrier((up3, down3, kv_own))
     far_a = lax.ppermute(up3[:half], "ctx", Z_UP)
     far_b = lax.ppermute(down3[half:], "ctx", Z_DOWN)
     kv_plane = plane_gather(kv_later)

time: 152 us -> 153 us (level)
  starting transfers between devices: 67.1 us -> 70.5 us
  waiting for transfers between devices: 38.8 us -> 36.8 us
    ppermute x1, starting transfers between devices: 0.01 us -> 3.77 us  [shards(): up2 = lax.ppermute(up1, 'ctx', Z_UP)]
    ppermute x1, starting transfers between devices: 4.2 us -> 0.65 us  [shards(): dkv_got = lax.ppermute(dkv_send, 'ctx', CORE_SWAP).astype(F32)]
    all_to_all x1, starting transfers between devices: 9.29 us -> 12.6 us  [shards(): lax.all_to_all(stats_sent, 'ctx', split_axis=0, concat_axis=0, tiled=True)]
    all_gather x1, waiting for transfers between devices: 6.03 us -> 8.23 us  [shards(): lax.all_gather(grads, 'ctx', axis=0, tiled=True, axis_index_groups=Z_GROUPS)]
    all_gather x1, waiting for transfers between devices: 2.08 us -> 0.02 us  [shards(): lax.all_gather(qg_sent, 'ctx', axis=0, tiled=True, axis_index_groups=Z_GR...]
    ppermute x1, waiting for transfers between devices: 2.97 us -> 1.12 us  [shards(): up1 = lax.ppermute(kv_own, 'ctx', Z_UP)]
  transfers between devices with their start and end apart: 37 -> 37, of which waited for: 17 -> 14; matrix products, arithmetic and copies ran while one was open for 4% -> 3% of each run, Pallas kernels for 10% -> 10%
where the time goes in v2:
time: 153 us; the launch traced here: 152 us
  starting transfers between devices  70.5 us (46%)
  waiting for transfers between devices  36.8 us (24%)
  Pallas kernels  19 us (12%)
  between operations  14.4 us (9%)
  local copies, waits for them, and re-layouts  8.53 us (6%)
  other arithmetic  3.12 us (2%)
    pallas_call x8, Pallas kernels, call(): pl.pallas_call(kernel, out_shape=out_shape, in_specs=specs, out_specs=jax...  19 us
    all_to_all x1, starting transfers between devices, shards(): lax.all_to_all(stats_sent, 'ctx', split_axis=0, concat_axis=0, tiled=True)  12.6 us
    ppermute x1, starting transfers between devices, shards(): moved_x = lax.ppermute(moved, 'tp', TP_X)  12.3 us
    all_gather x1, waiting for transfers between devices, shards(): lax.all_gather(grads, 'ctx', axis=0, tiled=True, axis_index_groups=Z_GROUPS)  8.23 us
    unnamed x18, local copies, waits for them, and re-layouts  5.82 us
    ppermute x3, waiting for transfers between devices, row_sum(): return mine + lax.ppermute(other, 'ctx', X_SWAP).astype(F32)  5.46 us
    ppermute x1, waiting for transfers between devices, shards(): n_up = lax.ppermute(pair, 'tp', TP_UP)  5.32 us
    ppermute x3, starting transfers between devices, row_sum(): got = lax.ppermute(send, 'ctx', CORE_SWAP).astype(F32)  4.14 us
  transfers between devices with their start and end apart: 37, of which 14 were waited for; matrix products, arithmetic and copies ran while one was open for 3% of the time, Pallas kernels for 10%

profile of v2, /device:TPU:1, one launch (start us, length us, event | category | flops | bytes accessed | tf_op | source)
XLA Modules:
  0.0 152.4 jit_solution(8160678545359841646)
XLA Ops:
  7.2 0.9 constant_dynamic-update-slice_fusion.1
  8.1 0.9 constant_dynamic-update-slice_fusion.refs_4_.refs_0_
  9.0 2.5 %collective-permute-start = (bf16[128,768]{1,0:T(8,128)(2,1)S(1)}, bf16[128,768]{1,0:T(8,128)(2,1)S(1)}, u32[]{:S(2)}, u32[]{:S(2)}) collective-permute-start(bf16[128,768]{1,0:T(8,128)(2,1)S(1)} %constant_dynamic-update-slice_fusion.refs_4_.refs_0_), channel_id=1, source_target_pairs={{0,32},{8,40},{16,48},{24,56},{32,64},{40,72},{48,80},{56,88},{64,... | collective-permute-start | bytes 589832 | tf_op jit(solution)/shard_map/ppermute | solution.py:285
  11.6 4.0 %collective-permute-start.1 = (bf16[128,768]{1,0:T(8,128)(2,1)S(1)}, bf16[128,768]{1,0:T(8,128)(2,1)S(1)}, u32[]{:S(2)}, u32[]{:S(2)}) collective-permute-start(bf16[128,768]{1,0:T(8,128)(2,1)S(1)} %constant_dynamic-update-slice_fusion.refs_4_.refs_0_), channel_id=1, source_target_pairs={{0,224},{8,232},{16,240},{24,248},{32,0},{40,8},{48,16},{56,24},{6... | collective-permute-start | bytes 589832 | tf_op jit(solution)/shard_map/ppermute | solution.py:286
  15.6 1.6 %collective-permute-start.2 = (bf16[128,640]{1,0:T(8,128)(2,1)}, bf16[128,640]{1,0:T(8,128)(2,1)S(1)}, u32[]{:S(2)}, u32[]{:S(2)}) collective-permute-start(bf16[128,640]{1,0:T(8,128)(2,1)} %param.6), channel_id=1, source_target_pairs={{0,0},{1,1},{2,2},{3,3},{4,4},{5,5},{6,6},{7,7},{8,8},{9,9},{10,10... | collective-permute-start | bytes 491528 | tf_op jit(solution)/shard_map/ppermute | solution.py:288
  17.2 0.9 constant_dynamic-update-slice_fusion.3
  18.1 0.9 constant_dynamic-update-slice_fusion.2
  19.0 1.1 collective-permute-done.refs_5_
  20.2 3.8 %collective-permute-start.3 = (bf16[128,768]{1,0:T(8,128)(2,1)S(1)}, bf16[128,768]{1,0:T(8,128)(2,1)S(1)}, u32[]{:S(2)}, u32[]{:S(2)}) collective-permute-start(bf16[128,768]{1,0:T(8,128)(2,1)S(1)} %collective-permute-done.refs_5_), channel_id=1, source_target_pairs={{0,32},{8,40},{16,48},{24,56},{32,64},{40,72},{48,80},{56,88},{64,... | collective-permute-start | bytes 589832 | tf_op jit(solution)/shard_map/ppermute | solution.py:293
  24.0 2.9 %collective-permute-start.4 = (bf16[128,768]{1,0:T(8,128)(2,1)S(1)}, bf16[128,768]{1,0:T(8,128)(2,1)S(1)}, u32[]{:S(2)}, u32[]{:S(2)}) collective-permute-start(bf16[128,768]{1,0:T(8,128)(2,1)S(1)} %collective-permute-done.1.refs_6_), channel_id=1, source_target_pairs={{0,224},{8,232},{16,240},{24,248},{32,0},{40,8},{48,16},{56,24},{6... | collective-permute-start | bytes 589832 | tf_op jit(solution)/shard_map/ppermute | solution.py:294
  27.2 2.7 %collective-permute-done.3.refs_7_ = bf16[128,768]{1,0:T(8,128)(2,1)S(1)} collective-permute-done((bf16[128,768]{1,0:T(8,128)(2,1)S(1)}, bf16[128,768]{1,0:T(8,128)(2,1)S(1)}, u32[]{:S(2)}, u32[]{:S(2)}) %collective-permute-start.3) | collective-permute-done | bytes 196640 | tf_op jit(solution)/shard_map/ppermute | solution.py:293
  30.5 2.1 %collective-permute-start.6 = (bf16[128,768]{1,0:T(8,128)(2,1)S(1)}, bf16[128,768]{1,0:T(8,128)(2,1)S(1)}, u32[]{:S(2)}, u32[]{:S(2)}) collective-permute-start(bf16[128,768]{1,0:T(8,128)(2,1)S(1)} %collective-permute-done.4.refs_8_), channel_id=1, source_target_pairs={{0,224},{8,232},{16,240},{24,248},{32,0},{40,8},{48,16},{56,24},{6... | collective-permute-start | bytes 589832 | tf_op jit(solution)/shard_map/ppermute | solution.py:297
  32.6 3.6 %collective-permute-start.10 = (bf16[128,768]{1,0:T(8,128)(2,1)}, bf16[128,768]{1,0:T(8,128)(2,1)S(1)}, u32[]{:S(2)}, u32[]{:S(2)}) collective-permute-start(bf16[128,768]{1,0:T(8,128)(2,1)} %copy-done.3), channel_id=1, source_target_pairs={{0,8},{8,0},{16,24},{24,16},{32,40},{40,32},{48,56},{56,48},{64,72... | collective-permute-start | bytes 589832 | tf_op jit(solution)/shard_map/ppermute | solution.py:253
  37.0 0.9 constant_dynamic-update-slice_fusion.5
  38.1 2.7 %collective-permute-start.14 = (bf16[64,768]{1,0:T(8,128)(2,1)S(1)}, bf16[64,768]{1,0:T(8,128)(2,1)S(1)}, u32[]{:S(2)}, u32[]{:S(2)}) collective-permute-start(bf16[64,768]{1,0:T(8,128)(2,1)S(1)} %slice.31), channel_id=1, source_target_pairs={{0,224},{8,232},{16,240},{24,248},{32,0},{40,8},{48,16},{56,24},{6... | collective-permute-start | bytes 294920 | tf_op jit(solution)/shard_map/ppermute | solution.py:300
  41.1 2.8 %near_statistics.1.refs_6_ = f32[8,512]{1,0:T(8,128)S(1)} custom-call(s32[20]{0:T(128)S(1)} %concatenate.19.place, bf16[128,768]{1,0:T(8,128)(2,1)S(1)} %constant_dynamic-update-slice_fusion.4.refs_0_, bf16[128,768]{1,0:T(8,128)(2,1)S(1)} %collective-permute-done.10.refs_1_, bf16[128,768]{1,0:T(8,128)(2,1)S(1)} %collective-permute-done.11.refs_2_, ...), custom_call_target="tpu_custom_call" | custom-call | flops 704643072 | bytes 2162768 | tf_op jit(solution)/shard_map/near_statistics/pallas_call | solution.py:235
  43.9 1.7 %softmax_statistics.1 = (f32[8,512]{1,0:T(8,128)S(1)}, f32[32,8,128]{2,1,0:T(8,128)}) custom-call(s32[20]{0:T(128)S(1)} %concatenate.19.place, bf16[128,768]{1,0:T(8,128)(2,1)S(1)} %constant_dynamic-update-slice_fusion.4.refs_0_, bf16[128,768]{1,0:T(8,128)(2,1)S(1)} %collective-permute-done.10.refs_1_, bf16[128,768]{1,0:T(8,128)(2,1)S(1)} %collective-permute-done.11.refs_2_, ...), custom_call_target="tpu_custom_call" | custom-call | flops 100663296 | bytes 999504 | tf_op jit(solution)/shard_map/softmax_statistics/pallas_call | solution.py:235
  45.7 12.6 %all-to-all-start = ((f32[32,8,128]{2,1,0:T(8,128)}), f32[32,8,128]{2,1,0:T(8,128)S(1)}, u32[]{:S(2)}, u32[]{:S(2)}) async-start(f32[32,8,128]{2,1,0:T(8,128)} %get-tuple-element.37), calls=%async_computation | async-start | bytes 262144 | tf_op jit(solution)/shard_map/all_to_all | solution.py:340
  59.4 1.5 collective-permute-start.16
  61.3 1.1 collective-permute-done.16.refs_15_
  62.4 2.1 %collective-permute-done.17.refs_16_ = f32[8,512]{1,0:T(8,128)S(1)} collective-permute-done((f32[8,512]{1,0:T(8,128)S(1)}, f32[8,512]{1,0:T(8,128)S(1)}, u32[]{:S(2)}, u32[]{:S(2)}) %collective-permute-start.17) | collective-permute-done | bytes 16416 | tf_op jit(solution)/shard_map/ppermute | solution.py:350
  64.5 3.7 %query_gradient.1 = (f32[2,128,384]{2,1,0:T(8,128)S(1)}, bf16[2,128,384]{2,1,0:T(8,128)(2,1)}) custom-call(s32[20]{0:T(128)S(1)} %concatenate.19.place, bf16[128,768]{1,0:T(8,128)(2,1)S(1)} %constant_dynamic-update-slice_fusion.4.refs_0_, bf16[128,768]{1,0:T(8,128)(2,1)S(1)} %collective-permute-done.10.refs_1_, ...), custom_call_target="tpu_custom_call" | custom-call | tf_op jit(solution)/shard_map/query_gradient/pallas_call | solution.py:235
  68.3 1.4 copy-done
  69.7 2.9 %core_gradient.1 = bf16[2,128,768]{2,1,0:T(8,128)(2,1)S(1)} custom-call(s32[20]{0:T(128)S(1)} %concatenate.19.place, bf16[128,768]{1,0:T(8,128)(2,1)S(1)} %collective-permute-done.7.refs_0_, bf16[128,768]{1,0:T(8,128)(2,1)S(1)} %collective-permute-done.9.refs_1_, bf16[1024,768]{1,0:T(8,128)(2,1)S(1)} %copy-done, f32[32,8,128]{2,1,0:T(8,128)S(1)} %all-to-all-done.refs_3_.refs_2_), custom_call_target="tpu_custom_call" | custom-call | flops 805306368 | bytes 2097232 | tf_op jit(solution)/shard_map/core_gradient/pallas_call | solution.py:235
  73.3 1.0 collective-permute-start.25
  74.4 1.8 %across_gradient.1 = f32[1,128,768]{2,1,0:T(8,128)S(1)} custom-call(s32[20]{0:T(128)S(1)} %concatenate.19.place, bf16[128,768]{1,0:T(8,128)(2,1)S(1)} %collective-permute-done.8.refs_0_, bf16[1024,768]{1,0:T(8,128)(2,1)S(1)} %copy-done, f32[32,8,128]{2,1,0:T(8,128)S(1)} %all-to-all-done.refs_3_.refs_2_), custom_call_target="tpu_custom_call" | custom-call | flops 402653184 | bytes 1900624 | tf_op jit(solution)/shard_map/across_gradient/pallas_call | solution.py:235
  76.9 0.9 collective-permute-done.25
  77.9 1.8 %own_gradient.1 = f32[1,128,768]{2,1,0:T(8,128)S(1)} custom-call(s32[20]{0:T(128)S(1)} %concatenate.19.place, bf16[128,768]{1,0:T(8,128)(2,1)S(1)} %constant_dynamic-update-slice_fusion.refs_4_.refs_0_, bf16[1024,768]{1,0:T(8,128)(2,1)S(1)} %copy-done.1, f32[32,8,128]{2,1,0:T(8,128)S(1)} %all-to-all-done.refs_3_.refs_2_), custom_call_target="tpu_custom_call" | custom-call | flops 402653184 | bytes 1900624 | tf_op jit(solution)/shard_map/own_gradient/pallas_call | solution.py:235
  79.7 2.9 %collective-permute-done.27 = bf16[128,768]{1,0:T(8,128)(2,1)S(1)} collective-permute-done((bf16[128,768]{1,0:T(8,128)(2,1)S(1)}, bf16[128,768]{1,0:T(8,128)(2,1)S(1)}, u32[]{:S(2)}, u32[]{:S(2)}) %collective-permute-start.27) | collective-permute-done | bytes 196640 | tf_op jit(solution)/shard_map/ppermute | solution.py:380
  82.7 0.7 pad_maximum_fusion
  84.1 12.3 %collective-permute-start.19 = (bf16[128,640]{1,0:T(8,128)(2,1)S(1)}, bf16[128,640]{1,0:T(8,128)(2,1)S(1)}, u32[]{:S(2)}, u32[]{:S(2)}) collective-permute-start(bf16[128,640]{1,0:T(8,128)(2,1)S(1)} %collective-permute-done.18), channel_id=1, source_target_pairs={{0,4},{1,5},{2,6},{3,7},{4,0},{5,1},{6,2},{7,3},{8,12},{9,13},{10,... | collective-permute-start | bytes 491528 | tf_op jit(solution)/shard_map/ppermute | solution.py:387
  96.4 2.7 %collective-permute-done.19 = bf16[128,640]{1,0:T(8,128)(2,1)S(1)} collective-permute-done((bf16[128,640]{1,0:T(8,128)(2,1)S(1)}, bf16[128,640]{1,0:T(8,128)(2,1)S(1)}, u32[]{:S(2)}, u32[]{:S(2)}) %collective-permute-start.19) | collective-permute-done | bytes 163872 | tf_op jit(solution)/shard_map/ppermute | solution.py:387
  99.1 1.1 collective-permute-start.20
  100.2 4.1 %collective-permute-start.21 = (bf16[256,640]{1,0:T(8,128)(2,1)S(1)}, bf16[256,640]{1,0:T(8,128)(2,1)S(1)}, u32[]{:S(2)}, u32[]{:S(2)}) collective-permute-start(bf16[256,640]{1,0:T(8,128)(2,1)S(1)} %constant_dynamic-update-slice_fusion.6.pair), channel_id=1, source_target_pairs={{0,3},{1,0},{2,1},{3,2},{4,7},{5,4},{6,5},{7,6},{8,11},{9,8},{10,9... | collective-permute-start | bytes 983048 | tf_op jit(solution)/shard_map/ppermute | solution.py:390
  104.3 5.3 %collective-permute-done.20.up = bf16[256,640]{1,0:T(8,128)(2,1)S(1)} collective-permute-done((bf16[256,640]{1,0:T(8,128)(2,1)S(1)}, bf16[256,640]{1,0:T(8,128)(2,1)S(1)}, u32[]{:S(2)}, u32[]{:S(2)}) %collective-permute-start.20) | collective-permute-done | bytes 327712 | tf_op jit(solution)/shard_map/ppermute | solution.py:389
  109.7 2.7 %collective-permute-start.23 = (bf16[128,640]{1,0:T(8,128)(2,1)S(1)}, bf16[128,640]{1,0:T(8,128)(2,1)S(1)}, u32[]{:S(2)}, u32[]{:S(2)}) collective-permute-start(bf16[128,640]{1,0:T(8,128)(2,1)S(1)} %slice.41), channel_id=1, source_target_pairs={{0,3},{1,0},{2,1},{3,2},{4,7},{5,4},{6,5},{7,6},{8,11},{9,8},{10,9... | collective-permute-start | bytes 491528 | tf_op jit(solution)/shard_map/ppermute | solution.py:399
  112.5 3.0 %collective-permute-done.22.up2 = bf16[128,640]{1,0:T(8,128)(2,1)S(1)} collective-permute-done((bf16[128,640]{1,0:T(8,128)(2,1)S(1)}, bf16[128,640]{1,0:T(8,128)(2,1)S(1)}, u32[]{:S(2)}, u32[]{:S(2)}) %collective-permute-start.22) | collective-permute-done | bytes 163872 | tf_op jit(solution)/shard_map/ppermute | solution.py:398
  115.5 1.0 normed_columns.1.at
  116.5 8.2 %all-gather.5.cloned.1.call-done.rows = bf16[1024,1152]{1,0:T(8,128)(2,1)} async-done(((bf16[128,1152]{1,0:T(8,128)(2,1)}), bf16[1024,1152]{1,0:T(8,128)(2,1)}) %all-gather.5.cloned.1.call-update) | async-done | bytes 2359312 | tf_op jit(solution)/shard_map/all_gather | solution.py:385
  124.7 1.7 %copy-done.2 = bf16[1024,1152]{1,0:T(8,128)(2,1)S(1)} copy-done((bf16[1024,1152]{1,0:T(8,128)(2,1)S(1)}, bf16[1024,1152]{1,0:T(8,128)(2,1)}, u32[]{:S(2)}) %copy-start.2) | copy-done | bytes 2359320
  126.4 3.3 %weight_product.1 = (f32[2,160,384]{2,1,0:T(8,128)S(1)}, bf16[2,160,384]{2,1,0:T(8,128)(2,1)S(1)}, f32[2,160,384]{2,1,0:T(8,128)S(1)}, bf16[2,160,384]{2,1,0:T(8...) custom-call(s32[20]{0:T(128)S(1)} %concatenate.19.place, ...), custom_call_target="tpu_custom_call" | custom-call | flops 1509949440 | bytes 3670096 | tf_op jit(solution)/shard_map/weight_product/pallas_call | solution.py:235
  129.6 3.6 %collective-permute-start.32 = (bf16[2,160,384]{2,1,0:T(8,128)(2,1)}, bf16[2,160,384]{2,1,0:T(8,128)(2,1)S(1)}, u32[]{:S(2)}, u32[]{:S(2)}) collective-permute-start(bf16[2,160,384]{2,1,0:T(8,128)(2,1)} %get-tuple-element.50), channel_id=1, source_target_pairs={{0,8},{8,0},{16,24},{24,16},{32,40},{40,32},{48,56},{56,48},{64,72... | collective-permute-start | bytes 737288 | tf_op jit(solution)/shard_map/ppermute | solution.py:259
  133.8 1.2 collective-permute-done.32
  135.0 1.3 collective-permute-start.33
  136.8 1.3 collective-permute-start.29
  138.1 1.5 %collective-permute-done.33 = bf16[160,384]{1,0:T(8,128)(2,1)S(1)} collective-permute-done((bf16[160,384]{1,0:T(8,128)(2,1)S(1)}, bf16[160,384]{1,0:T(8,128)(2,1)S(1)}, u32[]{:S(2)}, u32[]{:S(2)}) %collective-permute-start.33) | collective-permute-done | bytes 122912 | tf_op jit(solution)/shard_map/ppermute | solution.py:263
  140.3 2.0 %collective-permute-done.31 = bf16[160,384]{1,0:T(8,128)(2,1)S(1)} collective-permute-done((bf16[160,384]{1,0:T(8,128)(2,1)S(1)}, bf16[160,384]{1,0:T(8,128)(2,1)S(1)}, u32[]{:S(2)}, u32[]{:S(2)}) %collective-permute-start.31) | collective-permute-done | bytes 122912 | tf_op jit(solution)/shard_map/ppermute | solution.py:263
  143.0 2.0 %collective-permute-done.29 = bf16[160,384]{1,0:T(8,128)(2,1)S(1)} collective-permute-done((bf16[160,384]{1,0:T(8,128)(2,1)S(1)}, bf16[160,384]{1,0:T(8,128)(2,1)S(1)}, u32[]{:S(2)}, u32[]{:S(2)}) %collective-permute-start.29) | collective-permute-done | bytes 122912 | tf_op jit(solution)/shard_map/ppermute | solution.py:263
  (79 shorter events, 9.2 us)
Async XLA Ops:
  7.2 33.9 %copy-start.4 = (bf16[128,384]{1,0:T(8,128)(2,1)S(1)}, bf16[128,384]{1,0:T(8,128)(2,1)}, u32[]{:S(2)}) copy-start(bf16[128,384]{1,0:T(8,128)(2,1)} %param.10) | copy-start | bytes 294916
  7.2 61.1 %all-gather.3.cloned.1.call-start = ((), (), s32[]{:S(2)}) async-start(), calls=%async_computation.1 | async-start | bytes 1769472 | tf_op jit(solution)/shard_map/all_gather | solution.py:292
  9.0 11.1 %collective-permute-start = (bf16[128,768]{1,0:T(8,128)(2,1)S(1)}, bf16[128,768]{1,0:T(8,128)(2,1)S(1)}, u32[]{:S(2)}, u32[]{:S(2)}) collective-permute-start(bf16[128,768]{1,0:T(8,128)(2,1)S(1)} %constant_dynamic-update-slice_fusion.refs_4_.refs_0_), channel_id=1, source_target_pairs={{0,32},{8,40},{16,48},{24,56},{32,64},{40,72},{48,80},{56,88},{64,... | collective-permute-start | bytes 589832 | tf_op jit(solution)/shard_map/ppermute | solution.py:285
  11.6 8.6 %collective-permute-start.1 = (bf16[128,768]{1,0:T(8,128)(2,1)S(1)}, bf16[128,768]{1,0:T(8,128)(2,1)S(1)}, u32[]{:S(2)}, u32[]{:S(2)}) collective-permute-start(bf16[128,768]{1,0:T(8,128)(2,1)S(1)} %constant_dynamic-update-slice_fusion.refs_4_.refs_0_), channel_id=1, source_target_pairs={{0,224},{8,232},{16,240},{24,248},{32,0},{40,8},{48,16},{56,24},{6... | collective-permute-start | bytes 589832 | tf_op jit(solution)/shard_map/ppermute | solution.py:286
  15.6 3.4 %collective-permute-start.2 = (bf16[128,640]{1,0:T(8,128)(2,1)}, bf16[128,640]{1,0:T(8,128)(2,1)S(1)}, u32[]{:S(2)}, u32[]{:S(2)}) collective-permute-start(bf16[128,640]{1,0:T(8,128)(2,1)} %param.6), channel_id=1, source_target_pairs={{0,0},{1,1},{2,2},{3,3},{4,4},{5,5},{6,6},{7,7},{8,8},{9,9},{10,10... | collective-permute-start | bytes 491528 | tf_op jit(solution)/shard_map/ppermute | solution.py:288
  19.0 1.2 copy-start.3
  19.0 17.9 %copy-start.5 = (bf16[128,640]{1,0:T(8,128)(2,1)}, bf16[128,640]{1,0:T(8,128)(2,1)S(1)}, u32[]{:S(2)}) copy-start(bf16[128,640]{1,0:T(8,128)(2,1)S(1)} %collective-permute-done.2) | copy-start | bytes 491524
  20.2 9.6 %collective-permute-start.3 = (bf16[128,768]{1,0:T(8,128)(2,1)S(1)}, bf16[128,768]{1,0:T(8,128)(2,1)S(1)}, u32[]{:S(2)}, u32[]{:S(2)}) collective-permute-start(bf16[128,768]{1,0:T(8,128)(2,1)S(1)} %collective-permute-done.refs_5_), channel_id=1, source_target_pairs={{0,32},{8,40},{16,48},{24,56},{32,64},{40,72},{48,80},{56,88},{64,... | collective-permute-start | bytes 589832 | tf_op jit(solution)/shard_map/ppermute | solution.py:293
  24.0 5.9 %collective-permute-start.4 = (bf16[128,768]{1,0:T(8,128)(2,1)S(1)}, bf16[128,768]{1,0:T(8,128)(2,1)S(1)}, u32[]{:S(2)}, u32[]{:S(2)}) collective-permute-start(bf16[128,768]{1,0:T(8,128)(2,1)S(1)} %collective-permute-done.1.refs_6_), channel_id=1, source_target_pairs={{0,224},{8,232},{16,240},{24,248},{32,0},{40,8},{48,16},{56,24},{6... | collective-permute-start | bytes 589832 | tf_op jit(solution)/shard_map/ppermute | solution.py:294
  26.9 10.1 %collective-permute-start.11 = (bf16[128,768]{1,0:T(8,128)(2,1)}, bf16[128,768]{1,0:T(8,128)(2,1)S(1)}, u32[]{:S(2)}, u32[]{:S(2)}) collective-permute-start(bf16[128,768]{1,0:T(8,128)(2,1)} %copy-done.3), channel_id=1, source_target_pairs={{0,16},{8,24},{16,0},{24,8},{32,48},{40,56},{48,32},{56,40},{64,80... | collective-permute-start | bytes 589832 | tf_op jit(solution)/shard_map/ppermute | solution.py:252
  29.8 8.1 %collective-permute-start.5 = (bf16[128,768]{1,0:T(8,128)(2,1)S(1)}, bf16[128,768]{1,0:T(8,128)(2,1)S(1)}, u32[]{:S(2)}, u32[]{:S(2)}) collective-permute-start(bf16[128,768]{1,0:T(8,128)(2,1)S(1)} %collective-permute-done.3.refs_7_), channel_id=1, source_target_pairs={{0,32},{8,40},{16,48},{24,56},{32,64},{40,72},{48,80},{56,88},{64,... | collective-permute-start | bytes 589832 | tf_op jit(solution)/shard_map/ppermute | solution.py:296
  30.5 7.5 %collective-permute-start.6 = (bf16[128,768]{1,0:T(8,128)(2,1)S(1)}, bf16[128,768]{1,0:T(8,128)(2,1)S(1)}, u32[]{:S(2)}, u32[]{:S(2)}) collective-permute-start(bf16[128,768]{1,0:T(8,128)(2,1)S(1)} %collective-permute-done.4.refs_8_), channel_id=1, source_target_pairs={{0,224},{8,232},{16,240},{24,248},{32,0},{40,8},{48,16},{56,24},{6... | collective-permute-start | bytes 589832 | tf_op jit(solution)/shard_map/ppermute | solution.py:297
  32.6 8.5 %collective-permute-start.10 = (bf16[128,768]{1,0:T(8,128)(2,1)}, bf16[128,768]{1,0:T(8,128)(2,1)S(1)}, u32[]{:S(2)}, u32[]{:S(2)}) collective-permute-start(bf16[128,768]{1,0:T(8,128)(2,1)} %copy-done.3), channel_id=1, source_target_pairs={{0,8},{8,0},{16,24},{24,16},{32,40},{40,32},{48,56},{56,48},{64,72... | collective-permute-start | bytes 589832 | tf_op jit(solution)/shard_map/ppermute | solution.py:253
  36.9 4.2 %collective-permute-start.12 = (bf16[128,768]{1,0:T(8,128)(2,1)S(1)}, bf16[128,768]{1,0:T(8,128)(2,1)S(1)}, u32[]{:S(2)}, u32[]{:S(2)}) collective-permute-start(bf16[128,768]{1,0:T(8,128)(2,1)S(1)} %collective-permute-done.11.refs_2_), channel_id=1, source_target_pairs={{0,8},{8,0},{16,24},{24,16},{32,40},{40,32},{48,56},{56,48},{64,72... | collective-permute-start | bytes 589832 | tf_op jit(solution)/shard_map/ppermute | solution.py:254
  38.0 6.0 %collective-permute-start.13 = (bf16[64,768]{1,0:T(8,128)(2,1)S(1)}, bf16[64,768]{1,0:T(8,128)(2,1)S(1)}, u32[]{:S(2)}, u32[]{:S(2)}) collective-permute-start(bf16[64,768]{1,0:T(8,128)(2,1)S(1)} %slice.30), channel_id=1, source_target_pairs={{0,32},{8,40},{16,48},{24,56},{32,64},{40,72},{48,80},{56,88},{64,... | collective-permute-start | bytes 294920 | tf_op jit(solution)/shard_map/ppermute | solution.py:299
  38.1 5.9 %collective-permute-start.14 = (bf16[64,768]{1,0:T(8,128)(2,1)S(1)}, bf16[64,768]{1,0:T(8,128)(2,1)S(1)}, u32[]{:S(2)}, u32[]{:S(2)}) collective-permute-start(bf16[64,768]{1,0:T(8,128)(2,1)S(1)} %slice.31), channel_id=1, source_target_pairs={{0,224},{8,232},{16,240},{24,248},{32,0},{40,8},{48,16},{56,24},{6... | collective-permute-start | bytes 294920 | tf_op jit(solution)/shard_map/ppermute | solution.py:300
  40.8 18.1 %collective-permute-start.8 = (bf16[128,768]{1,0:T(8,128)(2,1)S(1)}, bf16[128,768]{1,0:T(8,128)(2,1)S(1)}, u32[]{:S(2)}, u32[]{:S(2)}) collective-permute-start(bf16[128,768]{1,0:T(8,128)(2,1)S(1)} %constant_dynamic-update-slice_fusion.refs_4_.refs_0_), channel_id=1, source_target_pairs={{0,16},{8,24},{16,0},{24,8},{32,48},{40,56},{48,32},{56,40},{64,80... | collective-permute-start | bytes 589832 | tf_op jit(solution)/shard_map/ppermute | solution.py:252
  45.7 22.6 %all-to-all-start = ((f32[32,8,128]{2,1,0:T(8,128)}), f32[32,8,128]{2,1,0:T(8,128)S(1)}, u32[]{:S(2)}, u32[]{:S(2)}) async-start(f32[32,8,128]{2,1,0:T(8,128)} %get-tuple-element.37), calls=%async_computation | async-start | bytes 262144 | tf_op jit(solution)/shard_map/all_to_all | solution.py:340
  58.3 66.4 %all-gather.5.cloned.1.call-start = ((), (), s32[]{:S(2)}) async-start(), calls=%async_computation.2 | async-start | bytes 2654208 | tf_op jit(solution)/shard_map/all_gather | solution.py:385
  58.3 9.9 %collective-permute-start.7 = (bf16[128,768]{1,0:T(8,128)(2,1)S(1)}, bf16[128,768]{1,0:T(8,128)(2,1)S(1)}, u32[]{:S(2)}, u32[]{:S(2)}) collective-permute-start(bf16[128,768]{1,0:T(8,128)(2,1)S(1)} %constant_dynamic-update-slice_fusion.refs_4_.refs_0_), channel_id=1, source_target_pairs={{0,8},{8,0},{16,24},{24,16},{32,40},{40,32},{48,56},{56,48},{64,72... | collective-permute-start | bytes 589832 | tf_op jit(solution)/shard_map/ppermute | solution.py:253
  58.8 9.4 %collective-permute-start.9 = (bf16[128,768]{1,0:T(8,128)(2,1)S(1)}, bf16[128,768]{1,0:T(8,128)(2,1)S(1)}, u32[]{:S(2)}, u32[]{:S(2)}) collective-permute-start(bf16[128,768]{1,0:T(8,128)(2,1)S(1)} %collective-permute-done.8.refs_0_), channel_id=1, source_target_pairs={{0,8},{8,0},{16,24},{24,16},{32,40},{40,32},{48,56},{56,48},{64,72... | collective-permute-start | bytes 589832 | tf_op jit(solution)/shard_map/ppermute | solution.py:254
  59.1 2.1 %collective-permute-start.15 = (f32[8,512]{1,0:T(8,128)S(1)}, f32[8,512]{1,0:T(8,128)S(1)}, u32[]{:S(2)}, u32[]{:S(2)}) collective-permute-start(f32[8,512]{1,0:T(8,128)S(1)} %get-tuple-element.38.refs_13_), channel_id=1, source_target_pairs={{0,8},{8,0},{16,24},{24,16},{32,40},{40,32},{48,56},{56,48},{64,72... | collective-permute-start | bytes 49160 | tf_op jit(solution)/shard_map/ppermute | solution.py:348
  59.4 3.0 %collective-permute-start.16 = (f32[8,512]{1,0:T(8,128)S(1)}, f32[8,512]{1,0:T(8,128)S(1)}, u32[]{:S(2)}, u32[]{:S(2)}) collective-permute-start(f32[8,512]{1,0:T(8,128)S(1)} %get-tuple-element.38.refs_13_), channel_id=1, source_target_pairs={{0,16},{8,24},{16,0},{24,8},{32,48},{40,56},{48,32},{56,40},{64,80... | collective-permute-start | bytes 49160 | tf_op jit(solution)/shard_map/ppermute | solution.py:349
  60.9 3.7 %collective-permute-start.17 = (f32[8,512]{1,0:T(8,128)S(1)}, f32[8,512]{1,0:T(8,128)S(1)}, u32[]{:S(2)}, u32[]{:S(2)}) collective-permute-start(f32[8,512]{1,0:T(8,128)S(1)} %get-tuple-element.38.refs_13_), channel_id=1, source_target_pairs={{0,24},{8,16},{16,8},{24,0},{32,56},{40,48},{48,40},{56,32},{64,88... | collective-permute-start | bytes 49160 | tf_op jit(solution)/shard_map/ppermute | solution.py:350
  68.3 5.0 %collective-permute-start.24 = (bf16[2,128,384]{2,1,0:T(8,128)(2,1)}, bf16[2,128,384]{2,1,0:T(8,128)(2,1)S(1)}, u32[]{:S(2)}, u32[]{:S(2)}) collective-permute-start(bf16[2,128,384]{2,1,0:T(8,128)(2,1)} %get-tuple-element.39), channel_id=1, source_target_pairs={{0,8},{8,0},{16,24},{24,16},{32,40},{40,32},{48,56},{56,48},{64,72... | collective-permute-start | bytes 589832 | tf_op jit(solution)/shard_map/ppermute | solution.py:356
  68.3 1.4 copy-start
  72.6 3.6 %collective-permute-start.26 = (bf16[2,128,768]{2,1,0:T(8,128)(2,1)S(1)}, bf16[2,128,768]{2,1,0:T(8,128)(2,1)S(1)}, u32[]{:S(2)}, u32[]{:S(2)}) collective-permute-start(bf16[2,128,768]{2,1,0:T(8,128)(2,1)S(1)} %core_gradient.1), channel_id=1, source_target_pairs={{0,8},{8,0},{16,24},{24,16},{32,40},{40,32},{48,56},{56,48},{64,72... | collective-permute-start | bytes 1179656 | tf_op jit(solution)/shard_map/ppermute | solution.py:378
  73.3 4.5 %collective-permute-start.25 = (bf16[128,384]{1,0:T(8,128)(2,1)S(1)}, bf16[128,384]{1,0:T(8,128)(2,1)S(1)}, u32[]{:S(2)}, u32[]{:S(2)}) collective-permute-start(bf16[128,384]{1,0:T(8,128)(2,1)S(1)} %fusion.15), channel_id=1, source_target_pairs={{0,16},{8,24},{16,0},{24,8},{32,48},{40,56},{48,32},{56,40},{64,80... | collective-permute-start | bytes 294920 | tf_op jit(solution)/shard_map/ppermute | solution.py:377
  76.2 1.7 %copy-start.1 = (bf16[1024,768]{1,0:T(8,128)(2,1)S(1)}, bf16[1024,768]{1,0:T(8,128)(2,1)}, u32[]{:S(2)}) copy-start(bf16[1024,768]{1,0:T(8,128)(2,1)} %all-gather.3.cloned.1.call-done.refs_2_.refs_1_) | copy-start | bytes 4718596
  76.3 6.3 %collective-permute-start.27 = (bf16[128,768]{1,0:T(8,128)(2,1)S(1)}, bf16[128,768]{1,0:T(8,128)(2,1)S(1)}, u32[]{:S(2)}, u32[]{:S(2)}) collective-permute-start(bf16[128,768]{1,0:T(8,128)(2,1)S(1)} %fusion.7), channel_id=1, source_target_pairs={{0,16},{8,24},{16,0},{24,8},{32,48},{40,56},{48,32},{56,40},{64,80... | collective-permute-start | bytes 589832 | tf_op jit(solution)/shard_map/ppermute | solution.py:380
  79.7 3.7 %copy-start.6 = (bf16[128,640]{1,0:T(8,128)(2,1)S(1)}, bf16[128,640]{1,0:T(8,128)(2,1)}, u32[]{:S(2)}) copy-start(bf16[128,640]{1,0:T(8,128)(2,1)} %copy-done.5) | copy-start | bytes 491524
  83.4 0.7 collective-permute-start.18
  84.1 15.0 %collective-permute-start.19 = (bf16[128,640]{1,0:T(8,128)(2,1)S(1)}, bf16[128,640]{1,0:T(8,128)(2,1)S(1)}, u32[]{:S(2)}, u32[]{:S(2)}) collective-permute-start(bf16[128,640]{1,0:T(8,128)(2,1)S(1)} %collective-permute-done.18), channel_id=1, source_target_pairs={{0,4},{1,5},{2,6},{3,7},{4,0},{5,1},{6,2},{7,3},{8,12},{9,13},{10,... | collective-permute-start | bytes 491528 | tf_op jit(solution)/shard_map/ppermute | solution.py:387
  99.1 10.5 %collective-permute-start.20 = (bf16[256,640]{1,0:T(8,128)(2,1)S(1)}, bf16[256,640]{1,0:T(8,128)(2,1)S(1)}, u32[]{:S(2)}, u32[]{:S(2)}) collective-permute-start(bf16[256,640]{1,0:T(8,128)(2,1)S(1)} %constant_dynamic-update-slice_fusion.6.pair), channel_id=1, source_target_pairs={{0,1},{1,2},{2,3},{3,0},{4,5},{5,6},{6,7},{7,4},{8,9},{9,10},{10,1... | collective-permute-start | bytes 983048 | tf_op jit(solution)/shard_map/ppermute | solution.py:389
  100.2 9.5 %collective-permute-start.21 = (bf16[256,640]{1,0:T(8,128)(2,1)S(1)}, bf16[256,640]{1,0:T(8,128)(2,1)S(1)}, u32[]{:S(2)}, u32[]{:S(2)}) collective-permute-start(bf16[256,640]{1,0:T(8,128)(2,1)S(1)} %constant_dynamic-update-slice_fusion.6.pair), channel_id=1, source_target_pairs={{0,3},{1,0},{2,1},{3,2},{4,7},{5,4},{6,5},{7,6},{8,11},{9,8},{10,9... | collective-permute-start | bytes 983048 | tf_op jit(solution)/shard_map/ppermute | solution.py:390
  109.6 5.9 %collective-permute-start.22 = (bf16[128,640]{1,0:T(8,128)(2,1)S(1)}, bf16[128,640]{1,0:T(8,128)(2,1)S(1)}, u32[]{:S(2)}, u32[]{:S(2)}) collective-permute-start(bf16[128,640]{1,0:T(8,128)(2,1)S(1)} %slice.40), channel_id=1, source_target_pairs={{0,1},{1,2},{2,3},{3,0},{4,5},{5,6},{6,7},{7,4},{8,9},{9,10},{10,1... | collective-permute-start | bytes 491528 | tf_op jit(solution)/shard_map/ppermute | solution.py:398
  109.7 5.7 %collective-permute-start.23 = (bf16[128,640]{1,0:T(8,128)(2,1)S(1)}, bf16[128,640]{1,0:T(8,128)(2,1)S(1)}, u32[]{:S(2)}, u32[]{:S(2)}) collective-permute-start(bf16[128,640]{1,0:T(8,128)(2,1)S(1)} %slice.41), channel_id=1, source_target_pairs={{0,3},{1,0},{2,1},{3,2},{4,7},{5,4},{6,5},{7,6},{8,11},{9,8},{10,9... | collective-permute-start | bytes 491528 | tf_op jit(solution)/shard_map/ppermute | solution.py:399
  124.7 1.7 %copy-start.2 = (bf16[1024,1152]{1,0:T(8,128)(2,1)S(1)}, bf16[1024,1152]{1,0:T(8,128)(2,1)}, u32[]{:S(2)}) copy-start(bf16[1024,1152]{1,0:T(8,128)(2,1)} %all-gather.5.cloned.1.call-done.rows) | copy-start | bytes 7077892
  129.6 5.3 %collective-permute-start.32 = (bf16[2,160,384]{2,1,0:T(8,128)(2,1)}, bf16[2,160,384]{2,1,0:T(8,128)(2,1)S(1)}, u32[]{:S(2)}, u32[]{:S(2)}) collective-permute-start(bf16[2,160,384]{2,1,0:T(8,128)(2,1)} %get-tuple-element.50), channel_id=1, source_target_pairs={{0,8},{8,0},{16,24},{24,16},{32,40},{40,32},{48,56},{56,48},{64,72... | collective-permute-start | bytes 737288 | tf_op jit(solution)/shard_map/ppermute | solution.py:259
  133.3 3.0 %collective-permute-start.30 = (bf16[2,160,384]{2,1,0:T(8,128)(2,1)S(1)}, bf16[2,160,384]{2,1,0:T(8,128)(2,1)S(1)}, u32[]{:S(2)}, u32[]{:S(2)}) collective-permute-start(bf16[2,160,384]{2,1,0:T(8,128)(2,1)S(1)} %get-tuple-element.48), channel_id=1, source_target_pairs={{0,8},{8,0},{16,24},{24,16},{32,40},{40,32},{48,56},{56,48},{64,72... | collective-permute-start | bytes 737288 | tf_op jit(solution)/shard_map/ppermute | solution.py:259
  133.3 3.5 %collective-permute-start.28 = (bf16[2,160,384]{2,1,0:T(8,128)(2,1)S(1)}, bf16[2,160,384]{2,1,0:T(8,128)(2,1)S(1)}, u32[]{:S(2)}, u32[]{:S(2)}) collective-permute-start(bf16[2,160,384]{2,1,0:T(8,128)(2,1)S(1)} %get-tuple-element.46), channel_id=1, source_target_pairs={{0,8},{8,0},{16,24},{24,16},{32,40},{40,32},{48,56},{56,48},{64,72... | collective-permute-start | bytes 737288 | tf_op jit(solution)/shard_map/ppermute | solution.py:259
  135.0 4.6 %collective-permute-start.33 = (bf16[160,384]{1,0:T(8,128)(2,1)S(1)}, bf16[160,384]{1,0:T(8,128)(2,1)S(1)}, u32[]{:S(2)}, u32[]{:S(2)}) collective-permute-start(bf16[160,384]{1,0:T(8,128)(2,1)S(1)} %fusion.14), channel_id=1, source_target_pairs={{0,16},{8,24},{16,0},{24,8},{32,48},{40,56},{48,32},{56,40},{64,80... | collective-permute-start | bytes 368648 | tf_op jit(solution)/shard_map/ppermute | solution.py:263
  136.4 5.9 %collective-permute-start.31 = (bf16[160,384]{1,0:T(8,128)(2,1)S(1)}, bf16[160,384]{1,0:T(8,128)(2,1)S(1)}, u32[]{:S(2)}, u32[]{:S(2)}) collective-permute-start(bf16[160,384]{1,0:T(8,128)(2,1)S(1)} %fusion.13), channel_id=1, source_target_pairs={{0,16},{8,24},{16,0},{24,8},{32,48},{40,56},{48,32},{56,40},{64,80... | collective-permute-start | bytes 368648 | tf_op jit(solution)/shard_map/ppermute | solution.py:263
  136.8 8.1 %collective-permute-start.29 = (bf16[160,384]{1,0:T(8,128)(2,1)S(1)}, bf16[160,384]{1,0:T(8,128)(2,1)S(1)}, u32[]{:S(2)}, u32[]{:S(2)}) collective-permute-start(bf16[160,384]{1,0:T(8,128)(2,1)S(1)} %fusion.12), channel_id=1, source_target_pairs={{0,16},{8,24},{16,0},{24,8},{32,48},{40,56},{48,32},{56,40},{64,80... | collective-permute-start | bytes 368648 | tf_op jit(solution)/shard_map/ppermute | solution.py:263
Sparse Core Ops, SparseCore 0:
  20.3 43.3 all-gather.2
  83.5 41.0 all-gather.4
